TPU v7x, 512 devices: a whole 4x4x16 slice. The times are simulated.
512 devices in a mesh: grp: 16 (over y, z_hi), dev: 32 (over z_lo, x, core).
Axes of the slice: x: 4, y: 4, z: 16 (z_hi: 4, z_lo: 4; z = z_hi * 4 + z_lo), core: 2. Of those that a mesh axis runs over, the one named last changes fastest.
Arguments:
- activations: bfloat16 [3584, 8192], P('grp', 'dev'), may hold values from -6 to 6
- cotangent: bfloat16 [3584, 4096], P('dev', 'grp'), may hold values from -6 to 6
- eigenbasis: bfloat16 [8192, 8192], P('dev'), may hold values from -0.0625 to 0.0625
- second_moment: bfloat16 [8192, 4096], P('dev', 'grp'), may hold values from 0.099609375 to 1
- factor: float32 [8192, 8192], P('grp', 'dev'), may hold values from -1 to 17, as said below
- old_panel: float32 [8192, 128], P('dev', 'grp'), may hold values from -6 to 6
Outputs:
- update: bfloat16 [8192, 4096], P('dev', 'grp')
- new_panel: float32 [8192, 128], P(('grp', 'dev'))
Inputs may be any that keep to these rules, and one draw needn't show every extreme that they name: `factor`: symmetric.
All inputs are finite; a program needn't handle non-finite values.
Results may differ from a plain program's by a relative error of at most 0.025.
Values may be sent and summed in bfloat16 or wider, within the bound.
A program may use at most 64 MiB of HBM per device.

v0:
```python
import jax
import jax.numpy as jnp
from jax import lax
from jax.sharding import PartitionSpec as P

D = 8192


damping = 0.01


def body(activations, cotangent, eigenbasis, second_moment, factor, old_panel):
    columns = eigenbasis
    rotated = lax.psum_scatter(
        lax.dot_general(
            columns, activations, (((0,), (1,)), ((), ())), preferred_element_type=jnp.float32
        ).astype(jnp.bfloat16),
        "dev",
        scatter_dimension=0,
        tiled=True,
    )
    all_tokens = lax.all_gather(rotated, "grp", axis=1, tiled=True)
    cot_rows = lax.all_gather(cotangent, "dev", axis=0, tiled=True)
    moment = jnp.dot(all_tokens, cot_rows, preferred_element_type=jnp.float32)
    scaled = (moment / all_tokens.shape[1] / (second_moment.astype(jnp.float32) + damping)).astype(
        jnp.bfloat16
    )
    columns = eigenbasis
    update = jnp.dot(
        columns,
        lax.all_gather(scaled, "dev", axis=0, tiled=True),
        preferred_element_type=jnp.float32,
    ).astype(jnp.bfloat16)
    local_rows = lax.all_gather(old_panel, "grp", axis=1, tiled=True)
    image_group = lax.psum(jnp.dot(factor, local_rows, precision=lax.Precision.HIGHEST), "dev")
    gram = lax.psum(jnp.dot(image_group.T, image_group, precision=lax.Precision.HIGHEST), "grp")
    share = image_group.shape[0] // lax.axis_size("dev")
    image = lax.dynamic_slice_in_dim(image_group, lax.axis_index("dev") * share, share, 0)
    gram = gram / D
    lower = jnp.linalg.cholesky(gram)
    new_panel = lax.linalg.triangular_solve(
        lower, image, left_side=False, lower=True, transpose_a=True
    )
    return (update, new_panel)


def solution(mesh):
    return jax.shard_map(
        body,
        mesh=mesh,
        in_specs=(
            P("grp", "dev"),
            P("dev", "grp"),
            P("dev", None),
            P("dev", "grp"),
            P("grp", "dev"),
            P("dev", "grp"),
        ),
        out_specs=(P("dev", "grp"), P(("grp", "dev"), None)),
        check_vma=False,
    )
```

profile of v0, /device:TPU:1, one launch (start us, length us, event | category | flops | bytes accessed | tf_op | source)
XLA Modules:
  0.0 884.5 jit_solution(13036835225285020874)
XLA Ops:
  7.2 0.0 copy-start
  7.2 0.0 copy-start.1
  7.2 0.0 reduce-scatter.2.cloned.1.call-start
  7.2 5.2 convolution_convert_fusion
  12.5 0.0 copy-start.2
  12.5 0.0 reduce-scatter.2.cloned.1.call-update
  12.5 0.0 all-reduce.3.cloned.1.call-start
  12.5 0.0 copy-done.1
  12.5 53.0 %all_gather.15 = f32[256,128]{0,1:T(8,128)S(1)} all-gather(f32[256,8]{0,1:T(8,128)S(1)} %copy-done.1), channel_id=1, replica_groups=mesh['grp'=16,'dev'=32] {'grp'}, dimensions={1}, use_global_device_ids=true | all-gather | bytes 139264 | tf_op jit(solution)/shard_map/all_gather | solution.py:34
  65.5 0.0 copy-done
  65.5 1.3 fusion.9
  66.8 0.0 all-reduce.3.cloned.1.call-update
  66.8 0.0 all-gather.6.cloned.1.call-start
  66.9 0.7 all-gather.6.cloned.1.call-update
  67.6 0.0 all-gather.4.cloned.1.call-start
  67.6 100.8 %reduce-scatter.2.cloned.1.call-done = bf16[256,224]{0,1:T(8,128)(2,1)} async-done(((bf16[8192,224]{0,1:T(8,128)(2,1)}), bf16[256,224]{0,1:T(8,128)(2,1)}) %reduce-scatter.2.cloned.1.call-update) | async-done | bytes 114704 | tf_op jit(solution)/shard_map/reduce_scatter | solution.py:14
  168.4 0.0 all-gather.4.cloned.1.call-update
  168.4 0.0 all-reduce.5.cloned.1.call-start
  168.4 287.8 %all-reduce.3.cloned.1.call-done = f32[512,128]{1,0:T(8,128)} async-done(((f32[512,128]{1,0:T(8,128)}), f32[512,128]{1,0:T(8,128)}) %all-reduce.3.cloned.1.call-update) | async-done | bytes 262160 | tf_op jit(solution)/shard_map/psum | solution.py:35
  456.3 2.2 fusion.10
  458.5 0.0 all-reduce.5.cloned.1.call-update
  458.5 0.0 all-gather.8.cloned.1.call-start
  458.6 64.1 %all-gather.6.cloned.1.call-done = bf16[3584,256]{1,0:T(8,128)(2,1)} async-done(((bf16[112,256]{1,0:T(8,128)(2,1)}), bf16[3584,256]{1,0:T(8,128)(2,1)}) %all-gather.6.cloned.1.call-update) | async-done | bytes 1835024 | tf_op jit(solution)/shard_map/all_gather | solution.py:23
  522.7 90.0 %all-gather.4.cloned.1.call-done = bf16[256,3584]{0,1:T(8,128)(2,1)} async-done(((bf16[256,224]{0,1:T(8,128)(2,1)}), bf16[256,3584]{0,1:T(8,128)(2,1)}) %all-gather.4.cloned.1.call-update) | async-done | bytes 1835024 | tf_op jit(solution)/shard_map/all_gather | solution.py:22
  612.6 0.0 copy-done.2
  612.6 3.4 fusion.1
  616.0 0.0 all-gather.8.cloned.1.call-update
  616.0 180.1 %all-reduce.5.cloned.1.call-done = f32[128,128]{0,1:T(8,128)} async-done(((f32[128,128]{0,1:T(8,128)}), f32[128,128]{0,1:T(8,128)}) %all-reduce.5.cloned.1.call-update) | async-done | bytes 65552 | tf_op jit(solution)/shard_map/psum | solution.py:36
  796.2 0.8 broadcast_multiply_fusion
  797.0 0.1 copy.12
  797.1 0.9 fusion.6
  798.0 11.7 %cholesky.16 = f32[128,128]{1,0:T(8,128)S(1)} custom-call(f32[128,128]{1,0:T(8,128)S(1)} %fusion.6), custom_call_target="Cholesky" | custom-call | tf_op jit(solution)/shard_map/jit(cholesky)/cholesky | solution.py:40
  809.7 0.6 compare_reduce_fusion
  810.4 0.7 fusion.3
  811.0 9.8 %custom-call.6 = f32[1,128,128]{1,2,0:T(8,128)S(1)} custom-call(f32[1,128,128]{2,1,0:T(8,128)S(1)} %fusion.3), custom_call_target="InvertDiagBlocksLowerTriangular" | custom-call | tf_op jit(solution)/shard_map/triangular_solve | solution.py:41
  820.8 1.5 fusion.4
  822.3 49.8 %all-gather.8.cloned.1.call-done = bf16[8192,256]{1,0:T(8,128)(2,1)} async-done(((bf16[256,256]{1,0:T(8,128)(2,1)}), bf16[8192,256]{1,0:T(8,128)(2,1)}) %all-gather.8.cloned.1.call-update) | async-done | bytes 4194320 | tf_op jit(solution)/shard_map/all_gather | solution.py:31
  872.1 4.8 fusion.2
  876.9 0.8 copy.13
  (1 shorter events, 0.0 us)
Async XLA Ops:
  7.2 58.4 %copy-start = (f32[512,256]{1,0:T(8,128)S(1)}, f32[512,256]{1,0:T(8,128)}, u32[]{:S(2)}) copy-start(f32[512,256]{1,0:T(8,128)} %param.10) | copy-start | bytes 1572868
  7.2 5.4 copy-start.1
  7.2 161.2 %reduce-scatter.2.cloned.1.call-start = ((), (), s32[]{:S(2)}) async-start(), calls=%async_computation.1 | async-start | bytes 3784704 | tf_op jit(solution)/shard_map/reduce_scatter | solution.py:14
  12.5 600.2 %copy-start.2 = (bf16[256,256]{1,0:T(8,128)(2,1)S(1)}, bf16[256,256]{1,0:T(8,128)(2,1)}, u32[]{:S(2)}) copy-start(bf16[256,256]{1,0:T(8,128)(2,1)} %param.9) | copy-start | bytes 393220
  12.5 443.8 %all-reduce.3.cloned.1.call-start = ((), (), s32[]{:S(2)}) async-start(), calls=%async_computation.5 | async-start | bytes 524288 | tf_op jit(solution)/shard_map/psum | solution.py:35
  66.8 455.8 %all-gather.6.cloned.1.call-start = ((), (), s32[]{:S(2)}) async-start(), calls=%async_computation.3 | async-start | bytes 1892352 | tf_op jit(solution)/shard_map/all_gather | solution.py:23
  67.6 545.0 %all-gather.4.cloned.1.call-start = ((), (), s32[]{:S(2)}) async-start(), calls=%async_computation.2 | async-start | bytes 1949696 | tf_op jit(solution)/shard_map/all_gather | solution.py:22
  168.4 627.8 %all-reduce.5.cloned.1.call-start = ((), (), s32[]{:S(2)}) async-start(), calls=%async_computation.6 | async-start | bytes 131072 | tf_op jit(solution)/shard_map/psum | solution.py:36
  458.5 413.6 %all-gather.8.cloned.1.call-start = ((), (), s32[]{:S(2)}) async-start(), calls=%async_computation.4 | async-start | bytes 4325376 | tf_op jit(solution)/shard_map/all_gather | solution.py:31
Sparse Core Ops, SparseCore 0:
  12.6 155.7 reduce-scatter.1
  171.5 284.7 all-reduce.2
  458.4 64.1 all-gather.5
  525.6 86.9 all-gather.3
  615.4 180.7 all-reduce.4
  799.0 73.1 all-gather.7
where the time goes:
time: 885 us; the launch traced here: 884 us
  waiting for transfers between devices  773 us (87%)
  blocking collectives  53 us (6%)
  other arithmetic  24.6 us (3%)
  matrix products  18.4 us (2%)
  between operations  14.2 us (2%)
    psum x1, waiting for transfers between devices, body(): lax.psum(jnp.dot(factor, local_rows, precision=lax.Precision.HIGHEST), 'd...  288 us
    psum x1, waiting for transfers between devices, body(): lax.psum(jnp.dot(image_group.T, image_group, precision=lax.Precision.HIGH...  180 us
    reduce_scatter x1, waiting for transfers between devices, body(): lax.psum_scatter(lax.dot_general(columns, activations, (((0,), (1,)), (()...  101 us
    all_gather x1, waiting for transfers between devices, body(): all_tokens = lax.all_gather(rotated, 'grp', axis=1, tiled=True)  90 us
    all_gather x1, waiting for transfers between devices, body(): cot_rows = lax.all_gather(cotangent, 'dev', axis=0, tiled=True)  64.1 us
    all_gather x1, blocking collectives, body(): local_rows = lax.all_gather(old_panel, 'grp', axis=1, tiled=True)  53 us
    all_gather x1, waiting for transfers between devices, body(): lax.all_gather(scaled, 'dev', axis=0, tiled=True)  49.8 us
  transfers between devices with their start and end apart: 6, of which 6 were waited for; matrix products, arithmetic and copies ran while one was open for 4% of the time, Pallas kernels for 0%

commit v1 on v0

v1 whole, which is shorter than its diff:
```python
import jax
import jax.numpy as jnp
from jax import lax
from jax.experimental import pallas as pl
from jax.experimental.pallas import tpu as pltpu
from jax.sharding import PartitionSpec as P

D = 8192
TOKENS = 3584
PANEL = 128
DAMPING = 0.01
MESH = pl.DeviceIdType.MESH
F32, BF16 = jnp.float32, jnp.bfloat16
HIGHEST = lax.Precision.HIGHEST

N_COPIES = 144


def dot(a, b, dims, precision=None):
    return lax.dot_general(a, b, (dims, ((), ())), precision=precision, preferred_element_type=F32)


def rel(i, o):
    return lax.rem(i + o, 4)


def kernel(
    a_ref, c_ref, q_hbm, v_ref, f_hbm, p_ref, upd_ref, new_ref,
    q, f, tok, cot, pan, scale, gt,
    send_c, recv_c, out2, recv2, out1p, out1m, recv1m, recv1p, out_z, recv_z, total, s, acc,
    im_part, im_c, im_s, im_x, im_xs, im_z,
    gr, gr_c, gr_h, gr_x, gr_q, gr_l, gr_l2, gr_y, gr_y2, gr_z, gr_full, chol_a, chol_b,
    send_sem, recv_sem, local_sem,
):
    grp, dev = lax.axis_index("grp"), lax.axis_index("dev")
    y, h = grp // 4, lax.rem(grp, 4)
    c = lax.rem(dev, 2)
    x = lax.rem(dev // 2, 4)
    z = dev // 8
    other = 1 - c

    def at(yy=y, hh=h, zz=z, xx=x, cc=c):
        return (yy * 4 + hh, (zz * 4 + xx) * 2 + cc)

    core_peer = at(cc=other)
    x_peer = {o: at(xx=rel(x, o)) for o in (1, 2, 3)}
    z_peer = {o: at(zz=rel(z, o)) for o in (1, 2, 3)}
    y_peer = {o: at(yy=rel(y, o)) for o in (1, 2, 3)}
    h_peer = {o: at(hh=rel(h, o)) for o in (1, 2, 3)}
    peers = [core_peer]
    for table in (x_peer, z_peer, y_peer, h_peer):
        peers += [table[o] for o in (1, 2, 3)]

    barrier = pltpu.get_barrier_semaphore()
    for peer in peers:
        pl.semaphore_signal(barrier, inc=1, device_id=peer, device_id_type=MESH)
    load_q = pltpu.make_async_copy(q_hbm, q, local_sem.at[0])
    load_f = pltpu.make_async_copy(f_hbm, f, local_sem.at[1])
    load_f.start()
    load_q.start()
    pl.semaphore_wait(barrier, len(peers))

    started = []

    def push(src, dst, peer):
        n = len(started)
        copy = pltpu.make_async_remote_copy(
            src_ref=src, dst_ref=dst, send_sem=send_sem.at[n], recv_sem=recv_sem.at[n],
            device_id=peer, device_id_type=MESH,
        )
        copy.start()
        started.append(copy)
        return copy

    pan_h = {o: push(p_ref, pan.at[h, y], h_peer[o]) for o in (1, 2, 3)}
    cot_x, cot_z, cot_f, cot_c = {}, {}, {}, {}
    for o in (2, 1, 3):
        cot_z[o] = push(c_ref, cot.at[x, z, c], z_peer[o])
    for o in (1, 3):
        cot_x[o, 0] = push(c_ref, cot.at[x, z, c], x_peer[o])
    tok_h, tok_y, tok_f = {}, {}, {}
    for o in (2, 1, 3):
        tok_h[o] = push(a_ref, tok.at[h, y], h_peer[o])
    for o in (1, 3):
        tok_y[o, 0] = push(a_ref, tok.at[h, y], y_peer[o])
    tok[h, y] = a_ref[...]
    cot[x, z, c] = c_ref[...]
    pan[h, y] = p_ref[...]
    scale[...] = (1.0 / TOKENS) / (v_ref[...].astype(F32) + DAMPING)

    for o in (1, 2, 3):
        pan_h[o].wait_recv()
    pan_y = {o: push(pan.at[:, y], pan.at[:, y], y_peer[o]) for o in (1, 2, 3)}

    for o in (1, 3, 2):
        cot_z[o].wait_recv()
        zz = rel(z, 4 - o)
        for ox in (1, 3):
            cot_x[ox, 4 - o] = push(cot.at[x, zz, c], cot.at[x, zz, c], x_peer[ox])
    cot_c[0] = push(cot.at[x, :, c], cot.at[x, :, c], core_peer)

    for o in (1, 2, 3):
        pan_y[o].wait_recv()
    load_f.wait()
    pan_t = pan[...].reshape(4, 4, 8, 256).transpose(1, 0, 2, 3).reshape(PANEL, 256)
    im_part[...] = dot(f[...], pan_t, ((1,), (1,)), HIGHEST).reshape(4, 4, 2, 16, PANEL)
    im_core = push(im_part.at[:, :, other], im_c, core_peer)

    for j in (0, 3, 1, 2):
        zz = rel(z, j)
        cot_x[1, j].wait_recv()
        if j in (0, 1):
            cot_f[j] = push(cot.at[rel(x, 3), zz, c], cot.at[rel(x, 3), zz, c], x_peer[1])
        cot_x[3, j].wait_recv()
        if j in (3, 2):
            cot_f[j] = push(cot.at[rel(x, 1), zz, c], cot.at[rel(x, 1), zz, c], x_peer[3])
    for o in (1, 3):
        cot_c[o] = push(cot.at[rel(x, o), :, c], cot.at[rel(x, o), :, c], core_peer)

    im_core.wait_recv()
    im_s[...] = im_part[:, :, c] + im_c[...]
    im_xc = {o: push(im_s.at[:, rel(x, o)], im_x.at[o], x_peer[o]) for o in (1, 2, 3)}

    for j in (0, 3, 1, 2):
        cot_f[j].wait_recv()
    cot_c[2] = push(cot.at[rel(x, 2), :, c], cot.at[rel(x, 2), :, c], core_peer)

    for o in (1, 2, 3):
        im_xc[o].wait_recv()
    im_xs[...] = im_s[:, x] + im_x[1] + im_x[2] + im_x[3]
    im_zc = {o: push(im_xs.at[rel(z, o)], im_z.at[o], z_peer[o]) for o in (1, 2, 3)}

    for o in (1, 3, 2):
        tok_h[o].wait_recv()
        hh = rel(h, 4 - o)
        for oy in (1, 3):
            tok_y[oy, 4 - o] = push(tok.at[hh, y], tok.at[hh, y], y_peer[oy])

    for o in (1, 2, 3):
        im_zc[o].wait_recv()
    image = im_xs[z] + im_z[1] + im_z[2] + im_z[3]
    gr[...] = dot(image, image, ((0,), (0,)), HIGHEST) * (1.0 / D)
    chol_b[...] = jnp.concatenate([image, jnp.zeros((PANEL - 16, PANEL), F32)], axis=0).T
    gr_core = push(gr.at[pl.ds(pl.multiple_of(other * 64, 64), 64)], gr_c, core_peer)

    for j in (0, 3, 1, 2):
        hh = rel(h, j)
        tok_y[1, j].wait_recv()
        if j in (0, 1):
            tok_f[j] = push(tok.at[hh, rel(y, 3)], tok.at[hh, rel(y, 3)], y_peer[1])
        tok_y[3, j].wait_recv()
        if j in (3, 2):
            tok_f[j] = push(tok.at[hh, rel(y, 1)], tok.at[hh, rel(y, 1)], y_peer[3])

    gr_core.wait_recv()
    gr_h[...] = gr[pl.ds(pl.multiple_of(c * 64, 64), 64), :] + gr_c[...]
    gr_xc = {
        o: push(gr_h.at[pl.ds(pl.multiple_of(rel(x, o) * 16, 16), 16)], gr_x.at[o], x_peer[o])
        for o in (1, 2, 3)
    }

    for j in (0, 3, 1, 2):
        tok_f[j].wait_recv()
    for o in (0, 1, 2, 3):
        cot_c[o].wait_recv()
    load_q.wait()

    gt[...] = dot(
        cot[...].reshape(TOKENS, 256), tok[...].reshape(TOKENS, 256), ((0,), (0,))
    ).astype(BF16)

    def block(ox, oz, cc):
        start = ((rel(z, oz) * 4 + rel(x, ox)) * 2 + cc) * 256
        return dot(gt[...], q[:, pl.ds(pl.multiple_of(start, 256), 256)], ((1,), (0,)))

    order = (2, 1, 3, 0)
    core = {}
    for ox in (2, 1, 3, 0):
        for j in range(4):
            send_c[ox, j] = block(ox, order[j], other).astype(BF16)
            core[ox, j] = push(send_c.at[ox, j], recv_c.at[ox, j], core_peer)

    def pair_sum(ox, j):
        own = block(ox, order[j], c)
        core[ox, j].wait_recv()
        return own + recv_c[ox, j].astype(F32)

    far, plus, minus, near = {}, {}, {}, {}

    def send_far(j):
        out2[j] = pair_sum(2, j).astype(BF16)
        far[j] = push(out2.at[j], recv2.at[j], x_peer[1 if j < 2 else 3])

    def send_plus(j):
        v = pair_sum(1, j)
        if j < 2:
            far[j].wait_recv()
            v = v + recv2[j].astype(F32)
        out1p[j] = v.astype(BF16)
        plus[j] = push(out1p.at[j], recv1m.at[j], x_peer[1])

    def send_minus(j):
        v = pair_sum(3, j)
        if j >= 2:
            far[j].wait_recv()
            v = v + recv2[j].astype(F32)
        out1m[j] = v.astype(BF16)
        minus[j] = push(out1m.at[j], recv1p.at[j], x_peer[3])

    send_far(0)
    send_minus(0)
    send_far(1)
    send_minus(1)
    send_far(2)
    send_far(3)
    for o in (1, 2, 3):
        gr_xc[o].wait_recv()
    gr_q[...] = gr_h[pl.ds(pl.multiple_of(x * 16, 16), 16), :] + gr_x[1] + gr_x[2] + gr_x[3]
    gr_zc = {o: push(gr_q, gr_l.at[o], z_peer[o]) for o in (1, 2, 3)}
    send_plus(0)
    send_plus(1)
    send_plus(2)
    send_minus(2)
    send_plus(3)
    send_minus(3)
    for o in (1, 2, 3):
        gr_zc[o].wait_recv()
    gr_l2[...] = gr_q[...] + gr_l[1] + gr_l[2] + gr_l[3]
    gr_yc = {o: push(gr_l2, gr_y.at[o], y_peer[o]) for o in (1, 2, 3)}

    for j in range(4):
        v = pair_sum(0, j)
        plus[j].wait_recv()
        v = v + recv1m[j].astype(F32)
        minus[j].wait_recv()
        v = v + recv1p[j].astype(F32)
        if order[j]:
            out_z[j] = v.astype(BF16)
            near[j] = push(out_z.at[j], recv_z.at[j], z_peer[order[j]])
        else:
            total[...] = v
        if j == 1:
            for o in (1, 2, 3):
                gr_yc[o].wait_recv()
            gr_y2[...] = gr_l2[...] + gr_y[1] + gr_y[2] + gr_y[3]
            gr_hc = {o: push(gr_y2, gr_z.at[o], h_peer[o]) for o in (1, 2, 3)}
    moment = total[...]
    for j in range(3):
        near[j].wait_recv()
        moment = moment + recv_z[j].astype(F32)
    s[0, 0, c] = (moment.T * scale[...]).astype(BF16)

    s_z, s_x, s_f, s_c = {}, {}, {}, {}
    mine = s.at[0, 0, c]
    for o in (2, 1, 3):
        s_z[o] = push(mine, s.at[0, 4 - o, c], z_peer[o])
    for o in (1, 3):
        s_x[o, 0] = push(mine, s.at[4 - o, 0, c], x_peer[o])
    s_c[0, 0] = push(mine, mine, core_peer)

    for o in (1, 2, 3):
        gr_hc[o].wait_recv()
    lo = pl.ds(pl.multiple_of(c * 64 + x * 16, 16), 16)
    gr_full[lo, :] = gr_y2[...] + gr_z[1] + gr_z[2] + gr_z[3]
    gr_xg = {o: push(gr_full.at[lo], gr_full.at[lo], x_peer[o]) for o in (1, 2, 3)}

    for o in (1, 3, 2):
        s_z[o].wait_recv()
        j = 4 - o
        for ox in (1, 3):
            s_x[ox, j] = push(s.at[0, j, c], s.at[4 - ox, j, c], x_peer[ox])
        s_c[0, j] = push(s.at[0, j, c], s.at[0, j, c], core_peer)

    for o in (1, 2, 3):
        gr_xg[o].wait_recv()
    half = pl.ds(pl.multiple_of(c * 64, 64), 64)
    gr_cg = push(gr_full.at[half], gr_full.at[half], core_peer)

    lane = lax.broadcasted_iota(jnp.int32, (8, PANEL), 1)
    row = lax.broadcasted_iota(jnp.int32, (8, PANEL), 0)

    def eliminate(b, carry):
        k0 = pl.multiple_of(b * 8, 8)
        r = chol_a[pl.ds(k0, 8), :]
        w = chol_b[pl.ds(k0, 8), :]
        r = pltpu.roll(r, lax.rem(PANEL - k0, PANEL), 1)
        for i in range(8):
            column = r[:, i : i + 1]
            pivot = column[i : i + 1, :]
            inv = lax.rsqrt(pivot)
            inv = inv * (1.5 - 0.5 * pivot * inv * inv)
            factor = column * inv
            r_row = r[i : i + 1, :] * inv
            w_row = w[i : i + 1, :] * inv
            r = jnp.where(row == i, r_row, jnp.where(row > i, r - factor * r_row, r))
            w = jnp.where(row == i, w_row, jnp.where(row > i, w - factor * w_row, w))
        r = pltpu.roll(r, k0, 1)
        r = jnp.where(lane >= k0 + 8, r, 0.0)
        chol_a[...] -= dot(r, r, ((0,), (0,)), HIGHEST)
        chol_b[...] -= dot(r, w, ((0,), (0,)), HIGHEST)
        chol_b[pl.ds(k0, 8), :] = w
        return carry

    def add_pair(ox, oz, first=False):
        start = ((rel(z, oz) * 4 + rel(x, ox)) * 2) * 256
        part = dot(
            q[:, pl.ds(pl.multiple_of(start, 512), 512)], s[ox, oz].reshape(512, 256), ((1,), (0,))
        )
        if first:
            acc[...] = part
        else:
            acc[...] += part

    gr_cg.wait_recv()
    chol_a[...] = gr_full[...]

    step = 0
    for j in (0, 3, 1, 2):
        s_x[1, j].wait_recv()
        if j in (0, 1):
            s_f[j] = push(s.at[3, j, c], s.at[2, j, c], x_peer[1])
        s_c[3, j] = push(s.at[3, j, c], s.at[3, j, c], core_peer)
        s_x[3, j].wait_recv()
        if j in (3, 2):
            s_f[j] = push(s.at[1, j, c], s.at[2, j, c], x_peer[3])
        s_c[1, j] = push(s.at[1, j, c], s.at[1, j, c], core_peer)
        s_c[0, j].wait_recv()
        add_pair(0, j, j == 0)
        lax.fori_loop(2 * step, 2 * step + 2, eliminate, 0)
        step += 1
    for j in (0, 3, 1, 2):
        s_f[j].wait_recv()
        s_c[2, j] = push(s.at[2, j, c], s.at[2, j, c], core_peer)
        for ox in (1, 3):
            s_c[ox, j].wait_recv()
            add_pair(ox, j)
        lax.fori_loop(2 * step, 2 * step + 2, eliminate, 0)
        step += 1
    new_ref[...] = chol_b[...].T[:16, :]
    for j in (0, 3, 1, 2):
        s_c[2, j].wait_recv()
        add_pair(2, j)
    upd_ref[...] = acc[...].astype(BF16)
    for copy in started:
        copy.wait_send()
    assert len(started) <= N_COPIES


def body(activations, cotangent, eigenbasis, second_moment, factor, old_panel):
    vmem = pl.BlockSpec(memory_space=pltpu.VMEM)
    hbm = pl.BlockSpec(memory_space=pl.ANY)
    tile = (256, 256)
    part = (16, PANEL)
    scratch = [
        pltpu.VMEM((256, D), BF16),
        pltpu.VMEM((512, 256), F32),
        pltpu.VMEM((4, 4, 224, 256), BF16),
        pltpu.VMEM((4, 4, 2, 112, 256), BF16),
        pltpu.VMEM((4, 4, 8, 256), F32),
        pltpu.VMEM(tile, F32),
        pltpu.VMEM(tile, BF16),
        pltpu.VMEM((4, 4) + tile, BF16),
        pltpu.VMEM((4, 4) + tile, BF16),
        pltpu.VMEM((4,) + tile, BF16),
        pltpu.VMEM((4,) + tile, BF16),
        pltpu.VMEM((4,) + tile, BF16),
        pltpu.VMEM((4,) + tile, BF16),
        pltpu.VMEM((4,) + tile, BF16),
        pltpu.VMEM((4,) + tile, BF16),
        pltpu.VMEM((4,) + tile, BF16),
        pltpu.VMEM((4,) + tile, BF16),
        pltpu.VMEM(tile, F32),
        pltpu.VMEM((4, 4, 2) + tile, BF16),
        pltpu.VMEM(tile, F32),
        pltpu.VMEM((4, 4, 2) + part, F32),
        pltpu.VMEM((4, 4) + part, F32),
        pltpu.VMEM((4, 4) + part, F32),
        pltpu.VMEM((4, 4) + part, F32),
        pltpu.VMEM((4,) + part, F32),
        pltpu.VMEM((4,) + part, F32),
        pltpu.VMEM((PANEL, PANEL), F32),
        pltpu.VMEM((64, PANEL), F32),
        pltpu.VMEM((64, PANEL), F32),
        pltpu.VMEM((4,) + part, F32),
        pltpu.VMEM(part, F32),
        pltpu.VMEM((4,) + part, F32),
        pltpu.VMEM(part, F32),
        pltpu.VMEM((4,) + part, F32),
        pltpu.VMEM(part, F32),
        pltpu.VMEM((4,) + part, F32),
        pltpu.VMEM((PANEL, PANEL), F32),
        pltpu.VMEM((PANEL, PANEL), F32),
        pltpu.VMEM((PANEL, PANEL), F32),
        pltpu.SemaphoreType.DMA((N_COPIES,)),
        pltpu.SemaphoreType.DMA((N_COPIES,)),
        pltpu.SemaphoreType.DMA((2,)),
    ]
    return pl.pallas_call(
        kernel,
        out_shape=(
            jax.ShapeDtypeStruct(tile, BF16),
            jax.ShapeDtypeStruct(part, F32),
        ),
        in_specs=[vmem, vmem, hbm, vmem, hbm, vmem],
        out_specs=(vmem, vmem),
        scratch_shapes=scratch,
        compiler_params=pltpu.CompilerParams(
            collective_id=0, has_side_effects=True, vmem_limit_bytes=48 * 1024 * 1024
        ),
    )(activations, cotangent, eigenbasis, second_moment, factor, old_panel.T)


def solution(mesh):
    return jax.shard_map(
        body,
        mesh=mesh,
        in_specs=(
            P("grp", "dev"),
            P("dev", "grp"),
            P("dev", None),
            P("dev", "grp"),
            P("grp", "dev"),
            P("dev", "grp"),
        ),
        out_specs=(P("dev", "grp"), P(("grp", "dev"), None)),
        check_vma=False,
    )
```

time: 885 us -> 142 us (0.16)
  waiting for transfers between devices: 773 us -> 0 us
  Pallas kernels: 0 us -> 131 us
  blocking collectives: 53 us -> 0 us
  other arithmetic: 24.6 us -> 0 us
  matrix products: 18.4 us -> 0 us
  between operations: 14.2 us -> 0.65 us
    psum x2 -> x0, waiting for transfers between devices: 468 us -> none  [the longest x1 288 us: body(): lax.psum(jnp.dot(factor, local_rows, precision=lax.Precision.HIGHEST), 'd...]
    all_gather x3 -> x0, waiting for transfers between devices: 204 us -> none  [the longest x1 90 us: body(): all_tokens = lax.all_gather(rotated, 'grp', axis=1, tiled=True)]
    pallas_call x0 -> x1, Pallas kernels: none -> 131 us  [body(): pl.pallas_call(kernel, out_shape=(jax.ShapeDtypeStruct(tile, BF16), jax.S...]
    reduce_scatter x1 -> x0, waiting for transfers between devices: 101 us -> none  [body(): lax.psum_scatter(lax.dot_general(columns, activations, (((0,), (1,)), (()...]
    all_gather x1 -> x0, blocking collectives: 53 us -> none  [body(): local_rows = lax.all_gather(old_panel, 'grp', axis=1, tiled=True)]
    another operation x5 -> x0, other arithmetic: 22.9 us -> none  [the longest x3 12.4 us: body(): lower = jnp.linalg.cholesky(gram)]
    dot_general x5 -> x0, matrix products: 16.9 us -> none  [the longest x1 5.22 us: body(): lax.dot_general(columns, activations, (((0,), (1,)), ((), ())), preferred...]
  transfers between devices with their start and end apart: 6 -> 0, of which waited for: 6 -> 0; matrix products, arithmetic and copies ran while one was open for 4% -> 0% of each run, Pallas kernels for 0% -> 0%
where the time goes in v1:
time: 142 us; the launch traced here: 140 us
  Pallas kernels  131 us (92%)
  local copies, waits for them, and re-layouts  7.79 us (5%)
    pallas_call x1, Pallas kernels, body(): pl.pallas_call(kernel, out_shape=(jax.ShapeDtypeStruct(tile, BF16), jax.S...  131 us
    unnamed x14, local copies, waits for them, and re-layouts  7.79 us

profile of v1, /device:TPU:1, one launch (start us, length us, event | category | flops | bytes accessed | tf_op | source)
XLA Modules:
  0.0 139.9 jit_solution(4869275080846622312)
XLA Ops:
  0.6 0.0 copy-start
  0.6 2.2 %copy-done = bf16[256,8192]{1,0:T(8,128)(2,1)S(1)} copy-done((bf16[256,8192]{1,0:T(8,128)(2,1)S(1)}, bf16[256,8192]{1,0:T(8,128)(2,1)}, u32[]{:S(2)}) %copy-start) | copy-done | bytes 4194328
  2.8 0.0 copy-start.1
  2.8 1.0 copy-done.1
  3.9 0.0 copy-start.2
  3.9 0.9 copy-done.2
  4.8 0.0 copy-start.3
  4.8 0.9 copy-done.3
  5.7 0.0 copy-start.4
  5.7 0.8 copy-done.4
  6.5 0.0 copy-start.5
  6.5 0.7 copy-done.5
  7.2 131.4 %shard_map.77 = (bf16[256,256]{1,0:T(8,128)(2,1)S(1)}, f32[16,128]{1,0:T(8,128)S(1)}) custom-call(bf16[224,256]{1,0:T(8,128)(2,1)S(1)} %copy-done.3, bf16[112,256]{1,0:T(8,128)(2,1)S(1)} %copy-done.4, bf16[256,8192]{1,0:T(8,128)(2,1)S(1)} %copy-done, bf16[256,256]{1,0:T(8,128)(2,1)S(1)} %copy-done.2, f32[512,256]{1,0:T(8,128)S(1)} %copy-done.1, ...), custom_call_target="tpu_custom_call" | custom-call | tf_op jit(solution)/shard_map/pallas_call | solution.py:398
  138.6 0.7 copy.10
  139.3 0.6 copy.11
Async XLA Ops:
  0.6 2.2 %copy-start = (bf16[256,8192]{1,0:T(8,128)(2,1)S(1)}, bf16[256,8192]{1,0:T(8,128)(2,1)}, u32[]{:S(2)}) copy-start(bf16[256,8192]{1,0:T(8,128)(2,1)} %q_hbm.1) | copy-start | bytes 12582916
  2.8 1.0 copy-start.1
  3.9 0.9 copy-start.2
  4.8 0.9 copy-start.3
  5.7 0.8 copy-start.4
  6.5 0.7 copy-start.5

commit v2 on v0

v2 whole, which is shorter than its diff:
```python
import jax
import jax.numpy as jnp
from jax import lax
from jax.experimental import pallas as pl
from jax.experimental.pallas import tpu as pltpu
from jax.sharding import PartitionSpec as P

D = 8192
TOKENS = 3584
PANEL = 128
DAMPING = 0.01
MESH = pl.DeviceIdType.MESH
F32, BF16 = jnp.float32, jnp.bfloat16
HIGHEST = lax.Precision.HIGHEST

N_COPIES = 176


def dot(a, b, dims, precision=None):
    return lax.dot_general(a, b, (dims, ((), ())), precision=precision, preferred_element_type=F32)


def rel(i, o):
    return lax.rem(i + o, 4)


def kernel(
    a_hbm, c_hbm, q_hbm, v_hbm, f_hbm, p_hbm, upd_ref, new_ref,
    q, f, v, tok, cot, pan, scale, gt_sum, gt,
    send_c, recv_c, out2, recv2, out1p, out1m, recv1m, recv1p, out_z, recv_z, total, s, acc,
    im_part, im_c, im_s, im_x, im_xs, im_z,
    gr, gr_c, gr_h, gr_x, gr_q, gr_l, gr_l2, gr_y, gr_y2, gr_z, gr_full, chol,
    send_sem, recv_sem, local_sem,
):
    grp, dev = lax.axis_index("grp"), lax.axis_index("dev")
    y, h = grp // 4, lax.rem(grp, 4)
    c = lax.rem(dev, 2)
    x = lax.rem(dev // 2, 4)
    z = dev // 8
    other = 1 - c

    def at(yy=y, hh=h, zz=z, xx=x, cc=c):
        return (yy * 4 + hh, (zz * 4 + xx) * 2 + cc)

    core_peer = at(cc=other)
    x_peer = {o: at(xx=rel(x, o)) for o in (1, 2, 3)}
    z_peer = {o: at(zz=rel(z, o)) for o in (1, 2, 3)}
    y_peer = {o: at(yy=rel(y, o)) for o in (1, 2, 3)}
    h_peer = {o: at(hh=rel(h, o)) for o in (1, 2, 3)}
    peers = [core_peer]
    for table in (x_peer, z_peer, y_peer, h_peer):
        peers += [table[o] for o in (1, 2, 3)]

    barrier = pltpu.get_barrier_semaphore()
    for peer in peers:
        pl.semaphore_signal(barrier, inc=1, device_id=peer, device_id_type=MESH)

    pairs = (
        (a_hbm, tok.at[h, y]), (c_hbm, cot.at[x, z, c]), (p_hbm, pan.at[h, y]),
        (v_hbm, v), (f_hbm, f), (q_hbm, q),
    )
    loads = [pltpu.make_async_copy(src, dst, local_sem.at[n]) for n, (src, dst) in enumerate(pairs)]
    for load in loads:
        load.start()
    for load in loads[:3]:
        load.wait()
    pl.semaphore_wait(barrier, len(peers))

    started, received = [], []

    def push(src, dst, peer):
        n = len(started)
        copy = pltpu.make_async_remote_copy(
            src_ref=src, dst_ref=dst, send_sem=send_sem.at[n], recv_sem=recv_sem.at[n],
            device_id=peer, device_id_type=MESH,
        )
        copy.start()
        started.append(copy)
        return copy

    def need(*copies):
        for copy in copies:
            assert id(copy) not in received
            received.append(id(copy))
            copy.wait_recv()

    def tok_push(hh, yy, k, peer):
        piece = tok.at[hh, yy, k]
        return push(piece, piece, peer)

    tok_h, tok_y, tok_yf = {}, {}, {}

    def tok_to_y(j, k):
        for o in (1, 3):
            tok_y[o, j, k] = tok_push(rel(h, j), y, k, y_peer[o])

    def tok_forward(j, k):
        o = (1, 3)[k]
        need(tok_y[o, j, k])
        tok_yf[j, k] = tok_push(rel(h, j), rel(y, 4 - o), k, y_peer[o])

    cot_x, cot_z, cot_f, cot_c = {}, {}, {}, {}

    def cot_push(xx, zz, peer):
        return push(cot.at[xx, zz, c], cot.at[xx, zz, c], peer)

    def cot_forward(j):
        zz = rel(z, j)
        need(cot_x[1, j], cot_x[3, j])
        o = 1 if j < 2 else 3
        cot_f[j] = cot_push(rel(x, 4 - o), zz, x_peer[o])

    def cot_pair(o):
        part = cot.at[rel(x, o), :, c]
        cot_c[o] = push(part, part, core_peer)

    pan_h = {o: push(pan.at[h, y], pan.at[h, y], h_peer[o]) for o in (2, 1, 3)}
    for o, k in ((1, 0), (3, 1)):
        tok_h[o, k] = tok_push(h, y, k, h_peer[o])
    for o in (2, 1, 3):
        cot_z[o] = cot_push(x, z, z_peer[o])
    for o, k in ((1, 1), (3, 0)):
        tok_h[o, k] = tok_push(h, y, k, h_peer[o])
    for k in (0, 1):
        tok_to_y(0, k)
    for o in (1, 3):
        cot_x[o, 0] = cot_push(x, z, x_peer[o])
    loads[3].wait()
    scale[...] = (1.0 / TOKENS) / (v[...].astype(F32) + DAMPING)

    tok_forward(0, 0)
    tok_forward(0, 1)
    need(*pan_h.values())
    pan_y = {o: push(pan.at[:, y], pan.at[:, y], y_peer[o]) for o in (2, 1, 3)}
    for o in (1, 3, 2):
        need(cot_z[o])
        for ox in (1, 3):
            cot_x[ox, 4 - o] = cot_push(x, rel(z, 4 - o), x_peer[ox])
    cot_pair(0)
    cot_forward(0)
    tok_hf = {}
    for o, k in ((1, 0), (3, 1)):
        need(tok_h[o, k])
        tok_hf[k] = tok_push(rel(h, 4 - o), y, k, h_peer[o])
        tok_to_y(4 - o, k)
    need(*pan_y.values())
    loads[4].wait()
    pan_t = pan[...].reshape(4, 4, 8, 256).transpose(1, 0, 2, 3).reshape(PANEL, 256)
    im_part[...] = dot(f[...], pan_t, ((1,), (1,)), HIGHEST).reshape(4, 4, 2, 16, PANEL)
    im_core = push(im_part.at[:, :, other], im_c, core_peer)
    for j in (3, 1, 2):
        cot_forward(j)
    cot_pair(1)
    cot_pair(3)
    tok_forward(3, 0)
    tok_forward(1, 1)
    need(im_core)
    im_s[...] = im_part[:, :, c] + im_c[...]
    im_xc = {o: push(im_s.at[:, rel(x, o)], im_x.at[o], x_peer[o]) for o in (1, 2, 3)}
    for o, k in ((1, 1), (3, 0)):
        need(tok_h[o, k])
        tok_to_y(4 - o, k)
    need(*cot_f.values())
    cot_pair(2)
    need(*im_xc.values())
    im_xs[...] = im_s[:, x] + im_x[1] + im_x[2] + im_x[3]
    im_zc = {o: push(im_xs.at[rel(z, o)], im_z.at[o], z_peer[o]) for o in (1, 2, 3)}
    for k in (0, 1):
        need(tok_hf[k])
        tok_to_y(2, k)
    tok_forward(3, 1)
    tok_forward(1, 0)
    need(*im_zc.values())
    image = im_xs[z] + im_z[1] + im_z[2] + im_z[3]
    gr[...] = dot(image, image, ((0,), (0,)), HIGHEST) * (1.0 / D)
    chol[:, PANEL:] = jnp.concatenate([image, jnp.zeros((PANEL - 16, PANEL), F32)], axis=0).T
    gr_core = push(gr.at[pl.ds(pl.multiple_of(other * 64, 64), 64)], gr_c, core_peer)
    tok_forward(2, 0)
    tok_forward(2, 1)
    need(*cot_c.values())
    need(gr_core)
    gr_h[...] = gr[pl.ds(pl.multiple_of(c * 64, 64), 64), :] + gr_c[...]
    gr_xc = {
        o: push(gr_h.at[pl.ds(pl.multiple_of(rel(x, o) * 16, 16), 16)], gr_x.at[o], x_peer[o])
        for o in (1, 2, 3)
    }

    for j in (0, 3, 1, 2):
        need(tok_y[3, j, 0], tok_y[1, j, 1], tok_yf[j, 0], tok_yf[j, 1])
        hh = rel(h, j)
        part = dot(cot[hh].reshape(896, 256), tok[hh].reshape(896, 256), ((0,), (0,)))
        if j == 0:
            gt_sum[...] = part
        elif j == 2:
            gt[...] = (gt_sum[...] + part).astype(BF16).reshape(2, 128, 256)
        else:
            gt_sum[...] += part
    loads[5].wait()

    order = (2, 1, 3, 0)

    def block(k, ox, j, cc):
        start = ((rel(z, order[j]) * 4 + rel(x, ox)) * 2 + cc) * 256
        return dot(gt[k], q[:, pl.ds(pl.multiple_of(start, 256), 256)], ((1,), (0,)))

    core, far, plus, minus, near = {}, {}, {}, {}, {}

    def send_core(k):
        for ox in (2, 3, 1, 0):
            for j in range(4):
                send_c[k, ox, j] = block(k, ox, j, other).astype(BF16)
            core[k, ox] = push(send_c.at[k, ox], recv_c.at[k, ox], core_peer)

    def pair_sum(k, ox, j):
        return block(k, ox, j, c) + recv_c[k, ox, j].astype(F32)

    def send_far(k, j):
        out2[k, j] = pair_sum(k, 2, j).astype(BF16)
        far[k, j] = push(out2.at[k, j], recv2.at[k, j], x_peer[1 if j < 2 else 3])

    def send_plus(k, j):
        total_j = pair_sum(k, 1, j)
        if j < 2:
            need(far[k, j])
            total_j = total_j + recv2[k, j].astype(F32)
        out1p[k, j] = total_j.astype(BF16)
        plus[k, j] = push(out1p.at[k, j], recv1m.at[k, j], x_peer[1])

    def send_minus(k, j):
        total_j = pair_sum(k, 3, j)
        if j >= 2:
            need(far[k, j])
            total_j = total_j + recv2[k, j].astype(F32)
        out1m[k, j] = total_j.astype(BF16)
        minus[k, j] = push(out1m.at[k, j], recv1p.at[k, j], x_peer[3])

    def send_first(k):
        need(core[k, 2])
        for j in (0, 2, 1, 3):
            send_far(k, j)
        need(core[k, 3])
        send_minus(k, 0)
        send_minus(k, 1)
        need(core[k, 1])
        send_plus(k, 2)
        send_plus(k, 3)

    def send_second(k):
        send_plus(k, 0)
        send_minus(k, 2)
        send_plus(k, 1)
        send_minus(k, 3)

    def send_z(k):
        need(core[k, 0])
        for j in range(4):
            total_j = pair_sum(k, 0, j)
            need(plus[k, j], minus[k, j])
            total_j = total_j + recv1m[k, j].astype(F32) + recv1p[k, j].astype(F32)
            if order[j]:
                out_z[k, j] = total_j.astype(BF16)
                near[k, j] = push(out_z.at[k, j], recv_z.at[k, j], z_peer[order[j]])
            else:
                total[k] = total_j

    s_z, s_x, s_f, s_c = {}, {}, {}, {}

    def gather_own(k):
        moment = total[k]
        for j in range(3):
            need(near[k, j])
            moment = moment + recv_z[k, j].astype(F32)
        s[k, 0, 0, c] = (moment.T * scale[:, k * 128 : (k + 1) * 128]).astype(BF16)
        mine = s.at[k, 0, 0, c]
        for o in (2, 1, 3):
            s_z[k, o] = push(mine, s.at[k, 0, 4 - o, c], z_peer[o])
        for o in (1, 3):
            s_x[k, o, 0] = push(mine, s.at[k, 4 - o, 0, c], x_peer[o])

    def gather_z(k, o):
        need(s_z[k, o])
        j = 4 - o
        for ox in (1, 3):
            s_x[k, ox, j] = push(s.at[k, 0, j, c], s.at[k, 4 - ox, j, c], x_peer[ox])

    def gather_pair(k, ox, lo, hi):
        part = s.at[k, ox, lo:hi, c]
        s_c[k, ox, lo] = push(part, part, core_peer)

    def gather_forward(k, j):
        need(s_x[k, 1, j], s_x[k, 3, j])
        o = 1 if j < 2 else 3
        s_f[k, j] = push(s.at[k, 4 - o, j, c], s.at[k, 2, j, c], x_peer[o])

    def add_blocks(k, ox, lo, hi):
        need(s_c[k, ox, lo])
        for j in range(lo, hi):
            start = ((rel(z, j) * 4 + rel(x, ox)) * 2) * 256
            part = dot(
                q[:, pl.ds(pl.multiple_of(start, 512), 512)],
                s[k, ox, j].reshape(512, 128),
                ((1,), (0,)),
            )
            if j == lo:
                sum_j = part
            else:
                sum_j = sum_j + part
        if ox == 0:
            acc[k] = sum_j
        else:
            acc[k] += sum_j

    lane = lax.broadcasted_iota(jnp.int32, (8, PANEL), 1)
    row = lax.broadcasted_iota(jnp.int32, (8, PANEL), 0)

    def eliminate(b):
        k0 = 8 * b
        r = chol[k0 : k0 + 8, :PANEL]
        w = chol[k0 : k0 + 8, PANEL:]
        for i in range(8):
            column = r[:, k0 + i : k0 + i + 1]
            pivot = column[i : i + 1, :]
            inv = lax.rsqrt(pivot)
            inv = inv * (1.5 - 0.5 * pivot * inv * inv)
            below = column * inv
            r_row = r[i : i + 1, :] * inv
            w_row = w[i : i + 1, :] * inv
            r = jnp.where(row == i, r_row, jnp.where(row > i, r - below * r_row, r))
            w = jnp.where(row == i, w_row, jnp.where(row > i, w - below * w_row, w))
        if b < 15:
            r = jnp.where(lane >= k0 + 8, r, 0.0)
            chol[...] -= dot(r, jnp.concatenate([r, w], axis=1), ((0,), (0,)), HIGHEST)
        chol[k0 : k0 + 8, PANEL:] = w

    send_core(0)
    send_first(0)
    need(*gr_xc.values())
    gr_q[...] = gr_h[pl.ds(pl.multiple_of(x * 16, 16), 16), :] + gr_x[1] + gr_x[2] + gr_x[3]
    gr_zc = {o: push(gr_q, gr_l.at[o], z_peer[o]) for o in (1, 2, 3)}
    send_core(1)
    send_second(0)
    need(*gr_zc.values())
    gr_l2[...] = gr_q[...] + gr_l[1] + gr_l[2] + gr_l[3]
    gr_yc = {o: push(gr_l2, gr_y.at[o], y_peer[o]) for o in (1, 2, 3)}
    send_first(1)
    need(*gr_yc.values())
    gr_y2[...] = gr_l2[...] + gr_y[1] + gr_y[2] + gr_y[3]
    gr_hc = {o: push(gr_y2, gr_z.at[o], h_peer[o]) for o in (1, 2, 3)}
    send_z(0)
    send_second(1)
    need(*gr_hc.values())
    lo = pl.ds(pl.multiple_of(c * 64 + x * 16, 16), 16)
    gr_full[lo, :] = gr_y2[...] + gr_z[1] + gr_z[2] + gr_z[3]
    gr_xg = {o: push(gr_full.at[lo], gr_full.at[lo], x_peer[o]) for o in (1, 2, 3)}
    send_z(1)
    gather_own(0)
    need(*gr_xg.values())
    half = pl.ds(pl.multiple_of(c * 64, 64), 64)
    gr_cg = push(gr_full.at[half], gr_full.at[half], core_peer)
    gather_own(1)
    need(gr_cg)
    chol[:, :PANEL] = gr_full[...]

    steps = iter(range(16))
    for k in (0, 1):
        for o in (1, 3, 2):
            gather_z(k, o)
            eliminate(next(steps))
        gather_pair(k, 0, 0, 4)
        for j in (0, 3, 1, 2):
            gather_forward(k, j)
            eliminate(next(steps))
        gather_pair(k, 1, 0, 4)
        gather_pair(k, 3, 0, 4)
        add_blocks(k, 0, 0, 4)
        if k == 1:
            for b in steps:
                eliminate(b)
            new_ref[...] = chol[:, PANEL:].T[:16, :]
            add_blocks(0, 1, 0, 4)
            add_blocks(0, 3, 0, 4)
    for k in (0, 1):
        need(s_f[k, 0], s_f[k, 1])
        gather_pair(k, 2, 0, 2)
        need(s_f[k, 2], s_f[k, 3])
        gather_pair(k, 2, 2, 4)
    add_blocks(1, 1, 0, 4)
    add_blocks(1, 3, 0, 4)
    for k in (0, 1):
        add_blocks(k, 2, 0, 2)
        add_blocks(k, 2, 2, 4)
        upd_ref[:, k * 128 : (k + 1) * 128] = acc[k].astype(BF16)
    for copy in started:
        copy.wait_send()
    assert len(started) <= N_COPIES
    assert len(started) == len(received)


def body(activations, cotangent, eigenbasis, second_moment, factor, old_panel):
    vmem = pl.BlockSpec(memory_space=pltpu.VMEM)
    hbm = pl.BlockSpec(memory_space=pl.ANY)
    tile = (128, 256)
    part = (16, PANEL)
    scratch = [
        pltpu.VMEM((256, D), BF16),
        pltpu.VMEM((512, 256), F32),
        pltpu.VMEM((256, 256), BF16),
        pltpu.VMEM((4, 4, 2, 112, 256), BF16),
        pltpu.VMEM((4, 4, 2, 112, 256), BF16),
        pltpu.VMEM((4, 4, 8, 256), F32),
        pltpu.VMEM((256, 256), F32),
        pltpu.VMEM((256, 256), F32),
        pltpu.VMEM((2,) + tile, BF16),
        pltpu.VMEM((2, 4, 4) + tile, BF16),
        pltpu.VMEM((2, 4, 4) + tile, BF16),
        pltpu.VMEM((2, 4) + tile, BF16),
        pltpu.VMEM((2, 4) + tile, BF16),
        pltpu.VMEM((2, 4) + tile, BF16),
        pltpu.VMEM((2, 4) + tile, BF16),
        pltpu.VMEM((2, 4) + tile, BF16),
        pltpu.VMEM((2, 4) + tile, BF16),
        pltpu.VMEM((2, 3) + tile, BF16),
        pltpu.VMEM((2, 3) + tile, BF16),
        pltpu.VMEM((2,) + tile, F32),
        pltpu.VMEM((2, 4, 4, 2, 256, 128), BF16),
        pltpu.VMEM((2, 256, 128), F32),
        pltpu.VMEM((4, 4, 2) + part, F32),
        pltpu.VMEM((4, 4) + part, F32),
        pltpu.VMEM((4, 4) + part, F32),
        pltpu.VMEM((4, 4) + part, F32),
        pltpu.VMEM((4,) + part, F32),
        pltpu.VMEM((4,) + part, F32),
        pltpu.VMEM((PANEL, PANEL), F32),
        pltpu.VMEM((64, PANEL), F32),
        pltpu.VMEM((64, PANEL), F32),
        pltpu.VMEM((4,) + part, F32),
        pltpu.VMEM(part, F32),
        pltpu.VMEM((4,) + part, F32),
        pltpu.VMEM(part, F32),
        pltpu.VMEM((4,) + part, F32),
        pltpu.VMEM(part, F32),
        pltpu.VMEM((4,) + part, F32),
        pltpu.VMEM((PANEL, PANEL), F32),
        pltpu.VMEM((PANEL, 2 * PANEL), F32),
        pltpu.SemaphoreType.DMA((N_COPIES,)),
        pltpu.SemaphoreType.DMA((N_COPIES,)),
        pltpu.SemaphoreType.DMA((6,)),
    ]
    return pl.pallas_call(
        kernel,
        out_shape=(
            jax.ShapeDtypeStruct((256, 256), BF16),
            jax.ShapeDtypeStruct(part, F32),
        ),
        in_specs=[hbm] * 6,
        out_specs=(vmem, vmem),
        scratch_shapes=scratch,
        compiler_params=pltpu.CompilerParams(
            collective_id=0, has_side_effects=True, vmem_limit_bytes=60 * 1024 * 1024
        ),
    )(
        activations.reshape(2, 112, 256), cotangent, eigenbasis, second_moment, factor, old_panel.T
    )


def solution(mesh):
    return jax.shard_map(
        body,
        mesh=mesh,
        in_specs=(
            P("grp", "dev"),
            P("dev", "grp"),
            P("dev", None),
            P("dev", "grp"),
            P("grp", "dev"),
            P("dev", "grp"),
        ),
        out_specs=(P("dev", "grp"), P(("grp", "dev"), None)),
        check_vma=False,
    )
```

time: 885 us -> 118 us (0.13)
  waiting for transfers between devices: 773 us -> 0 us
  Pallas kernels: 0 us -> 114 us
  blocking collectives: 53 us -> 0 us
  other arithmetic: 24.6 us -> 0 us
  matrix products: 18.4 us -> 0 us
  between operations: 14.2 us -> 0.64 us
    psum x2 -> x0, waiting for transfers between devices: 468 us -> none  [the longest x1 288 us: body(): lax.psum(jnp.dot(factor, local_rows, precision=lax.Precision.HIGHEST), 'd...]
    all_gather x3 -> x0, waiting for transfers between devices: 204 us -> none  [the longest x1 90 us: body(): all_tokens = lax.all_gather(rotated, 'grp', axis=1, tiled=True)]
    pallas_call x0 -> x1, Pallas kernels: none -> 114 us  [body(): pl.pallas_call(kernel, out_shape=(jax.ShapeDtypeStruct((256, 256), BF16),...]
    reduce_scatter x1 -> x0, waiting for transfers between devices: 101 us -> none  [body(): lax.psum_scatter(lax.dot_general(columns, activations, (((0,), (1,)), (()...]
    all_gather x1 -> x0, blocking collectives: 53 us -> none  [body(): local_rows = lax.all_gather(old_panel, 'grp', axis=1, tiled=True)]
    another operation x5 -> x0, other arithmetic: 22.9 us -> none  [the longest x3 12.4 us: body(): lower = jnp.linalg.cholesky(gram)]
    dot_general x5 -> x0, matrix products: 16.9 us -> none  [the longest x1 5.22 us: body(): lax.dot_general(columns, activations, (((0,), (1,)), ((), ())), preferred...]
  transfers between devices with their start and end apart: 6 -> 0, of which waited for: 6 -> 0; matrix products, arithmetic and copies ran while one was open for 4% -> 0% of each run, Pallas kernels for 0% -> 0%
where the time goes in v2:
time: 118 us; the launch traced here: 117 us
  Pallas kernels  114 us (97%)
  local copies, waits for them, and re-layouts  2.86 us (2%)
    pallas_call x1, Pallas kernels, body(): pl.pallas_call(kernel, out_shape=(jax.ShapeDtypeStruct((256, 256), BF16),...  114 us
    unnamed x2, local copies, waits for them, and re-layouts  2.86 us

profile of v2, /device:TPU:1, one launch (start us, length us, event | category | flops | bytes accessed | tf_op | source)
XLA Modules:
  0.0 117.2 jit_solution(3507270447651780533)
XLA Ops:
  0.6 113.7 %shard_map.77 = (bf16[256,256]{1,0:T(8,128)(2,1)}, f32[16,128]{1,0:T(8,128)}) custom-call(bf16[2,112,256]{2,1,0:T(8,128)(2,1)} %bitcast.2, bf16[112,256]{1,0:T(8,128)(2,1)} %c_hbm.1, bf16[256,8192]{1,0:T(8,128)(2,1)} %q_hbm.1, bf16[256,256]{1,0:T(8,128)(2,1)} %v_hbm.1, f32[512,256]{1,0:T(8,128)} %f_hbm.1, f32[8,256]{1,0:T(8,128)} %bitcast.3), custom_call_target="tpu_custom_call" | custom-call | tf_op jit(solution)/shard_map/pallas_call | solution.py:449
  114.4 1.6 %copy.10 = bf16[256,256]{1,0:T(8,128)(2,1)} copy(bf16[256,256]{1,0:T(8,128)(2,1)} %get-tuple-element.4) | data formatting | bytes 262144
  115.9 1.3 %copy.11 = f32[16,128]{1,0:T(8,128)} copy(f32[16,128]{1,0:T(8,128)} %get-tuple-element.5) | data formatting | bytes 16384

commit v3 on v2

v3 whole, which is shorter than its diff:
```python
import jax
import jax.numpy as jnp
from jax import lax
from jax.experimental import pallas as pl
from jax.experimental.pallas import tpu as pltpu
from jax.sharding import PartitionSpec as P

D = 8192
TOKENS = 3584
PANEL = 128
DAMPING = 0.01
MESH = pl.DeviceIdType.MESH
F32, BF16 = jnp.float32, jnp.bfloat16
HIGHEST = lax.Precision.HIGHEST

N_COPIES = 176


def dot(a, b, dims, precision=None):
    return lax.dot_general(a, b, (dims, ((), ())), precision=precision, preferred_element_type=F32)


def rel(i, o):
    return lax.rem(i + o, 4)


def kernel(
    a_hbm, c_hbm, q_hbm, v_hbm, f_hbm, p_hbm, upd_ref, new_ref,
    q, f, v, act, rot, cot, pan, scale, moment,
    send_c, recv_c, out2, recv2, out1p, out1m, recv1m, recv1p, out_z, recv_z, total, s, acc,
    im_part, im_c, im_s, im_x, im_xs, im_z,
    gr, gr_c, gr_h, gr_x, gr_q, gr_l, gr_l2, gr_y, gr_y2, gr_z, gr_full, chol,
    send_sem, recv_sem, local_sem,
):
    grp, dev = lax.axis_index("grp"), lax.axis_index("dev")
    y, h = grp // 4, lax.rem(grp, 4)
    c = lax.rem(dev, 2)
    x = lax.rem(dev // 2, 4)
    z = dev // 8
    other = 1 - c

    def at(yy=y, hh=h, zz=z, xx=x, cc=c):
        return (yy * 4 + hh, (zz * 4 + xx) * 2 + cc)

    core_peer = at(cc=other)
    x_peer = {o: at(xx=rel(x, o)) for o in (1, 2, 3)}
    z_peer = {o: at(zz=rel(z, o)) for o in (1, 2, 3)}
    y_peer = {o: at(yy=rel(y, o)) for o in (1, 2, 3)}
    h_peer = {o: at(hh=rel(h, o)) for o in (1, 2, 3)}
    peers = [core_peer]
    for table in (x_peer, z_peer, y_peer, h_peer):
        peers += [table[o] for o in (1, 2, 3)]

    barrier = pltpu.get_barrier_semaphore()
    for peer in peers:
        pl.semaphore_signal(barrier, inc=1, device_id=peer, device_id_type=MESH)

    pairs = (
        (p_hbm, pan.at[h, y]), (c_hbm, cot.at[x, z, c]), (a_hbm, act), (q_hbm, q),
        (f_hbm, f), (v_hbm, v),
    )
    loads = [pltpu.make_async_copy(src, dst, local_sem.at[n]) for n, (src, dst) in enumerate(pairs)]
    for load in loads:
        load.start()
    for load in loads[:2]:
        load.wait()
    pl.semaphore_wait(barrier, len(peers))

    started, received = [], []

    def push(src, dst, peer):
        n = len(started)
        copy = pltpu.make_async_remote_copy(
            src_ref=src, dst_ref=dst, send_sem=send_sem.at[n], recv_sem=recv_sem.at[n],
            device_id=peer, device_id_type=MESH,
        )
        copy.start()
        started.append(copy)
        return copy

    def need(*copies):
        for copy in copies:
            assert id(copy) not in received
            received.append(id(copy))
            copy.wait_recv()

    cot_x, cot_z, cot_f, cot_c = {}, {}, {}, {}

    def cot_push(xx, zz, peer):
        return push(cot.at[xx, zz, c], cot.at[xx, zz, c], peer)

    def cot_forward(j):
        zz = rel(z, j)
        need(cot_x[1, j], cot_x[3, j])
        o = 1 if j < 2 else 3
        cot_f[j] = cot_push(rel(x, 4 - o), zz, x_peer[o])

    def cot_pair(o):
        part = cot.at[rel(x, o), :, c]
        cot_c[o] = push(part, part, core_peer)

    order = (2, 1, 3, 0)

    def columns(k, oz, ox, cc):
        start = ((rel(z, oz) * 4 + rel(x, ox)) * 2 + cc) * 256 + k * 128
        return q[:, pl.ds(pl.multiple_of(start, 128), 128)]

    def block(k, ox, j, cc):
        return dot(act[...], columns(k, order[j], ox, cc), ((1,), (0,)))

    core, far, plus, minus, near = {}, {}, {}, {}, {}

    def send_core(k):
        for ox in (2, 3, 1, 0):
            for j in range(4):
                send_c[k, ox, j] = block(k, ox, j, other).astype(BF16)
            core[k, ox] = push(send_c.at[k, ox], recv_c.at[k, ox], core_peer)

    def pair_sum(k, ox, j):
        return block(k, ox, j, c) + recv_c[k, ox, j].astype(F32)

    def send_far(k, j):
        out2[k, j] = pair_sum(k, 2, j).astype(BF16)
        far[k, j] = push(out2.at[k, j], recv2.at[k, j], x_peer[1 if j < 2 else 3])

    def send_plus(k, j):
        total_j = pair_sum(k, 1, j)
        if j < 2:
            need(far[k, j])
            total_j = total_j + recv2[k, j].astype(F32)
        out1p[k, j] = total_j.astype(BF16)
        plus[k, j] = push(out1p.at[k, j], recv1m.at[k, j], x_peer[1])

    def send_minus(k, j):
        total_j = pair_sum(k, 3, j)
        if j >= 2:
            need(far[k, j])
            total_j = total_j + recv2[k, j].astype(F32)
        out1m[k, j] = total_j.astype(BF16)
        minus[k, j] = push(out1m.at[k, j], recv1p.at[k, j], x_peer[3])

    def send_first(k):
        need(core[k, 2])
        for j in (0, 2, 1, 3):
            send_far(k, j)
        need(core[k, 3])
        send_minus(k, 0)
        send_minus(k, 1)
        need(core[k, 1])
        send_plus(k, 2)
        send_plus(k, 3)

    def send_second(k):
        send_plus(k, 0)
        send_minus(k, 2)
        send_plus(k, 1)
        send_minus(k, 3)

    def send_z(k):
        need(core[k, 0])
        for j in range(4):
            total_j = pair_sum(k, 0, j)
            need(plus[k, j], minus[k, j])
            total_j = total_j + recv1m[k, j].astype(F32) + recv1p[k, j].astype(F32)
            if order[j]:
                out_z[k, j] = total_j.astype(BF16)
                near[k, j] = push(out_z.at[k, j], recv_z.at[k, j], z_peer[order[j]])
            else:
                total[k] = total_j

    rot_h, rot_hf, rot_y = {}, {}, {}

    def rot_to_y(k, j):
        block_j = rot.at[k, rel(h, j), y]
        for o in (2, 1, 3):
            rot_y[k, o, j] = push(block_j, block_j, y_peer[o])

    def rot_own(k):
        sum_k = total[k]
        for j in range(3):
            need(near[k, j])
            sum_k = sum_k + recv_z[k, j].astype(F32)
        rot[k, h, y] = sum_k.astype(BF16)
        for o in (1, 3):
            rot_h[k, o] = push(rot.at[k, h, y], rot.at[k, h, y], h_peer[o])
        rot_to_y(k, 0)

    def rot_next(k):
        for o in (1, 3):
            need(rot_h[k, o])
            lo = 0 if o == 1 else 112
            part = rot.at[k, rel(h, 4 - o), y, lo : lo + 112]
            rot_hf[k, o] = push(part, part, h_peer[o])
            rot_to_y(k, 4 - o)

    def rot_last(k):
        need(rot_hf[k, 1], rot_hf[k, 3])
        rot_to_y(k, 2)

    def add_tokens(k, j):
        need(rot_y[k, 1, j], rot_y[k, 2, j], rot_y[k, 3, j])
        hh = rel(h, j)
        part = dot(rot[k, hh].reshape(896, 128), cot[hh].reshape(896, 256), ((0,), (0,)))
        if j == 0:
            moment[k] = part
        else:
            moment[k] += part

    s_z, s_x, s_f, s_c = {}, {}, {}, {}

    def gather_own(k):
        s[k, 0, 0, c] = (moment[k] * scale[k * 128 : (k + 1) * 128, :]).astype(BF16)
        mine = s.at[k, 0, 0, c]
        for o in (2, 1, 3):
            s_z[k, o] = push(mine, s.at[k, 0, 4 - o, c], z_peer[o])
        for o in (1, 3):
            s_x[k, o, 0] = push(mine, s.at[k, 4 - o, 0, c], x_peer[o])

    def gather_z(k, o):
        need(s_z[k, o])
        j = 4 - o
        for ox in (1, 3):
            s_x[k, ox, j] = push(s.at[k, 0, j, c], s.at[k, 4 - ox, j, c], x_peer[ox])

    def gather_pair(k, ox, lo, hi):
        part = s.at[k, ox, lo:hi, c]
        s_c[k, ox, lo] = push(part, part, core_peer)

    def gather_forward(k, j):
        need(s_x[k, 1, j], s_x[k, 3, j])
        o = 1 if j < 2 else 3
        s_f[k, j] = push(s.at[k, 4 - o, j, c], s.at[k, 2, j, c], x_peer[o])

    def add_blocks(k, ox, lo, hi):
        need(s_c[k, ox, lo])
        sum_j = jnp.zeros((256, 256), F32)
        for j in range(lo, hi):
            for cc in (0, 1):
                sum_j = sum_j + dot(columns(k, j, ox, cc), s[k, ox, j, cc], ((1,), (0,)))
        if k == 0 and ox == 0:
            acc[...] = sum_j
        else:
            acc[...] += sum_j

    lane = lax.broadcasted_iota(jnp.int32, (8, PANEL), 1)
    row = lax.broadcasted_iota(jnp.int32, (8, PANEL), 0)

    def eliminate(b):
        k0 = 8 * b
        r = chol[k0 : k0 + 8, :PANEL]
        w = chol[k0 : k0 + 8, PANEL:]
        for i in range(8):
            column = r[:, k0 + i : k0 + i + 1]
            pivot = column[i : i + 1, :]
            inv = lax.rsqrt(pivot)
            inv = inv * (1.5 - 0.5 * pivot * inv * inv)
            below = column * inv
            r_row = r[i : i + 1, :] * inv
            w_row = w[i : i + 1, :] * inv
            r = jnp.where(row == i, r_row, jnp.where(row > i, r - below * r_row, r))
            w = jnp.where(row == i, w_row, jnp.where(row > i, w - below * w_row, w))
        if b < 15:
            r = jnp.where(lane >= k0 + 8, r, 0.0)
            chol[...] -= dot(r, jnp.concatenate([r, w], axis=1), ((0,), (0,)), HIGHEST)
        chol[k0 : k0 + 8, PANEL:] = w

    def panel_y():
        need(*pan_h.values())
        return {o: push(pan.at[:, y], pan.at[:, y], y_peer[o]) for o in (2, 1, 3)}

    def image_core():
        need(*pan_y.values())
        loads[4].wait()
        pan_t = pan[...].transpose(1, 0, 2, 3).reshape(PANEL, 256)
        im_part[...] = dot(f[...], pan_t, ((1,), (1,)), HIGHEST).reshape(4, 4, 2, 16, PANEL)
        return push(im_part.at[:, :, other], im_c, core_peer)

    def image_x():
        need(im_core)
        im_s[...] = im_part[:, :, c] + im_c[...]
        return {o: push(im_s.at[:, rel(x, o)], im_x.at[o], x_peer[o]) for o in (1, 2, 3)}

    def image_z():
        need(*im_xc.values())
        im_xs[...] = im_s[:, x] + im_x[1] + im_x[2] + im_x[3]
        return {o: push(im_xs.at[rel(z, o)], im_z.at[o], z_peer[o]) for o in (1, 2, 3)}

    def gram_core():
        need(*im_zc.values())
        image = im_xs[z] + im_z[1] + im_z[2] + im_z[3]
        gr[...] = dot(image, image, ((0,), (0,)), HIGHEST) * (1.0 / D)
        chol[:, PANEL:] = jnp.concatenate([image, jnp.zeros((PANEL - 16, PANEL), F32)], axis=0).T
        return push(gr.at[pl.ds(pl.multiple_of(other * 64, 64), 64)], gr_c, core_peer)

    def gram_x():
        need(gr_core)
        gr_h[...] = gr[pl.ds(pl.multiple_of(c * 64, 64), 64), :] + gr_c[...]
        return {
            o: push(
                gr_h.at[pl.ds(pl.multiple_of(rel(x, o) * 16, 16), 16)], gr_x.at[o], x_peer[o]
            )
            for o in (1, 2, 3)
        }

    def gram_z():
        need(*gr_xc.values())
        mine = gr_h[pl.ds(pl.multiple_of(x * 16, 16), 16), :]
        gr_q[...] = mine + gr_x[1] + gr_x[2] + gr_x[3]
        return {o: push(gr_q, gr_l.at[o], z_peer[o]) for o in (1, 2, 3)}

    def gram_y():
        need(*gr_zc.values())
        gr_l2[...] = gr_q[...] + gr_l[1] + gr_l[2] + gr_l[3]
        return {o: push(gr_l2, gr_y.at[o], y_peer[o]) for o in (1, 2, 3)}

    def gram_h():
        need(*gr_yc.values())
        gr_y2[...] = gr_l2[...] + gr_y[1] + gr_y[2] + gr_y[3]
        return {o: push(gr_y2, gr_z.at[o], h_peer[o]) for o in (1, 2, 3)}

    def gram_x_back():
        need(*gr_hc.values())
        lo = pl.ds(pl.multiple_of(c * 64 + x * 16, 16), 16)
        gr_full[lo, :] = gr_y2[...] + gr_z[1] + gr_z[2] + gr_z[3]
        return {o: push(gr_full.at[lo], gr_full.at[lo], x_peer[o]) for o in (1, 2, 3)}

    def gram_core_back():
        need(*gr_xg.values())
        half = pl.ds(pl.multiple_of(c * 64, 64), 64)
        return push(gr_full.at[half], gr_full.at[half], core_peer)

    pan_h = {o: push(pan.at[h, y], pan.at[h, y], h_peer[o]) for o in (2, 1, 3)}
    for o in (2, 1, 3):
        cot_z[o] = cot_push(x, z, z_peer[o])
    loads[2].wait()
    loads[3].wait()
    send_core(0)
    send_first(0)
    send_core(1)
    loads[5].wait()
    scale[...] = (1.0 / TOKENS) / (v[...].astype(F32) + DAMPING)
    send_second(0)
    pan_y = panel_y()
    send_first(1)
    im_core = image_core()
    send_z(0)
    im_xc = image_x()
    send_second(1)
    for o in (1, 3):
        cot_x[o, 0] = cot_push(x, z, x_peer[o])
    for o in (1, 3, 2):
        need(cot_z[o])
        for ox in (1, 3):
            cot_x[ox, 4 - o] = cot_push(x, rel(z, 4 - o), x_peer[ox])
    cot_pair(0)
    im_zc = image_z()
    rot_own(0)
    send_z(1)
    gr_core = gram_core()
    for j in (0, 3, 1, 2):
        cot_forward(j)
    cot_pair(1)
    cot_pair(3)
    gr_xc = gram_x()
    rot_next(0)
    rot_own(1)
    need(*cot_f.values())
    cot_pair(2)
    gr_zc = gram_z()
    rot_last(0)
    rot_next(1)
    gr_yc = gram_y()
    need(*cot_c.values())
    for j in (0, 3, 1, 2):
        add_tokens(0, j)
    gather_own(0)
    rot_last(1)
    gr_hc = gram_h()
    gather_z(0, 1)
    gather_z(0, 3)
    gather_z(0, 2)
    gather_pair(0, 0, 0, 4)
    for j in (0, 3, 1, 2):
        add_tokens(1, j)
    gather_own(1)
    gr_xg = gram_x_back()
    gather_forward(0, 0)
    gather_forward(0, 3)
    gr_cg = gram_core_back()
    gather_forward(0, 1)
    gather_forward(0, 2)
    gather_pair(0, 1, 0, 4)
    gather_pair(0, 3, 0, 4)
    need(gr_cg)
    chol[:, :PANEL] = gr_full[...]
    steps = iter(range(16))
    add_blocks(0, 0, 0, 4)
    eliminate(next(steps))
    for o in (1, 3, 2):
        gather_z(1, o)
        eliminate(next(steps))
    gather_pair(1, 0, 0, 4)
    add_blocks(0, 1, 0, 4)
    add_blocks(0, 3, 0, 4)
    need(s_f[0, 0], s_f[0, 1])
    gather_pair(0, 2, 0, 2)
    need(s_f[0, 2], s_f[0, 3])
    gather_pair(0, 2, 2, 4)
    for j in (0, 3, 1, 2):
        eliminate(next(steps))
        gather_forward(1, j)
    gather_pair(1, 1, 0, 4)
    gather_pair(1, 3, 0, 4)
    add_blocks(0, 2, 0, 2)
    add_blocks(0, 2, 2, 4)
    add_blocks(1, 0, 0, 4)
    for b in steps:
        eliminate(b)
    need(s_f[1, 0], s_f[1, 1])
    gather_pair(1, 2, 0, 2)
    need(s_f[1, 2], s_f[1, 3])
    gather_pair(1, 2, 2, 4)
    new_ref[...] = chol[:, PANEL:].T[:16, :]
    add_blocks(1, 1, 0, 4)
    add_blocks(1, 3, 0, 4)
    add_blocks(1, 2, 0, 2)
    add_blocks(1, 2, 2, 4)
    upd_ref[...] = acc[...].astype(BF16)
    for copy in started:
        copy.wait_send()
    assert len(started) <= N_COPIES
    assert len(started) == len(received)


def body(activations, cotangent, eigenbasis, second_moment, factor, old_panel):
    vmem = pl.BlockSpec(memory_space=pltpu.VMEM)
    hbm = pl.BlockSpec(memory_space=pl.ANY)
    tile = (224, 128)
    half = (128, 256)
    part = (16, PANEL)
    scratch = [
        pltpu.VMEM((256, D), BF16),
        pltpu.VMEM((512, 256), F32),
        pltpu.VMEM((256, 256), BF16),
        pltpu.VMEM((224, 256), BF16),
        pltpu.VMEM((2, 4, 4) + tile, BF16),
        pltpu.VMEM((4, 4, 2, 112, 256), BF16),
        pltpu.VMEM((4, 4, 8, 256), F32),
        pltpu.VMEM((256, 256), F32),
        pltpu.VMEM((2,) + half, F32),
        pltpu.VMEM((2, 4, 4) + tile, BF16),
        pltpu.VMEM((2, 4, 4) + tile, BF16),
        pltpu.VMEM((2, 4) + tile, BF16),
        pltpu.VMEM((2, 4) + tile, BF16),
        pltpu.VMEM((2, 4) + tile, BF16),
        pltpu.VMEM((2, 4) + tile, BF16),
        pltpu.VMEM((2, 4) + tile, BF16),
        pltpu.VMEM((2, 4) + tile, BF16),
        pltpu.VMEM((2, 3) + tile, BF16),
        pltpu.VMEM((2, 3) + tile, BF16),
        pltpu.VMEM((2,) + tile, F32),
        pltpu.VMEM((2, 4, 4, 2) + half, BF16),
        pltpu.VMEM((256, 256), F32),
        pltpu.VMEM((4, 4, 2) + part, F32),
        pltpu.VMEM((4, 4) + part, F32),
        pltpu.VMEM((4, 4) + part, F32),
        pltpu.VMEM((4, 4) + part, F32),
        pltpu.VMEM((4,) + part, F32),
        pltpu.VMEM((4,) + part, F32),
        pltpu.VMEM((PANEL, PANEL), F32),
        pltpu.VMEM((64, PANEL), F32),
        pltpu.VMEM((64, PANEL), F32),
        pltpu.VMEM((4,) + part, F32),
        pltpu.VMEM(part, F32),
        pltpu.VMEM((4,) + part, F32),
        pltpu.VMEM(part, F32),
        pltpu.VMEM((4,) + part, F32),
        pltpu.VMEM(part, F32),
        pltpu.VMEM((4,) + part, F32),
        pltpu.VMEM((PANEL, PANEL), F32),
        pltpu.VMEM((PANEL, 2 * PANEL), F32),
        pltpu.SemaphoreType.DMA((N_COPIES,)),
        pltpu.SemaphoreType.DMA((N_COPIES,)),
        pltpu.SemaphoreType.DMA((6,)),
    ]
    return pl.pallas_call(
        kernel,
        out_shape=(
            jax.ShapeDtypeStruct((256, 256), BF16),
            jax.ShapeDtypeStruct(part, F32),
        ),
        in_specs=[hbm] * 6,
        out_specs=(vmem, vmem),
        scratch_shapes=scratch,
        compiler_params=pltpu.CompilerParams(
            collective_id=0, has_side_effects=True, vmem_limit_bytes=60 * 1024 * 1024
        ),
    )(
        activations, cotangent, eigenbasis, second_moment, factor, old_panel.T
    )


def solution(mesh):
    return jax.shard_map(
        body,
        mesh=mesh,
        in_specs=(
            P("grp", "dev"),
            P("dev", "grp"),
            P("dev", None),
            P("dev", "grp"),
            P("grp", "dev"),
            P("dev", "grp"),
        ),
        out_specs=(P("dev", "grp"), P(("grp", "dev"), None)),
        check_vma=False,
    )
```

time: 118 us -> 105 us (0.89)
  the two profiles are of different devices: /device:TPU:1 before, /device:TPU:93 now
where the time goes in v3:
time: 105 us
  Pallas kernels  101 us (96%)
  local copies, waits for them, and re-layouts  2.86 us (3%)
    pallas_call x1, Pallas kernels, body(): pl.pallas_call(kernel, out_shape=(jax.ShapeDtypeStruct((256, 256), BF16),...  101 us
    unnamed x2, local copies, waits for them, and re-layouts  2.86 us

profile of v3, /device:TPU:93, one launch (start us, length us, event | category | flops | bytes accessed | tf_op | source)
XLA Modules:
  0.0 104.7 jit_solution(13747796228735697962)
XLA Ops:
  0.6 101.2 %shard_map.77 = (bf16[256,256]{1,0:T(8,128)(2,1)}, f32[16,128]{1,0:T(8,128)}) custom-call(bf16[224,256]{1,0:T(8,128)(2,1)} %a_hbm.1, bf16[112,256]{1,0:T(8,128)(2,1)} %c_hbm.1, bf16[256,8192]{1,0:T(8,128)(2,1)} %q_hbm.1, bf16[256,256]{1,0:T(8,128)(2,1)} %v_hbm.1, f32[512,256]{1,0:T(8,128)} %f_hbm.1, f32[8,256]{1,0:T(8,128)} %bitcast.1), custom_call_target="tpu_custom_call" | custom-call | tf_op jit(solution)/shard_map/pallas_call | solution.py:486
  101.8 1.6 %copy.10 = bf16[256,256]{1,0:T(8,128)(2,1)} copy(bf16[256,256]{1,0:T(8,128)(2,1)} %get-tuple-element.4) | data formatting | bytes 262144
  103.4 1.3 %copy.11 = f32[16,128]{1,0:T(8,128)} copy(f32[16,128]{1,0:T(8,128)} %get-tuple-element.5) | data formatting | bytes 16384

commit v4 on v3

v4 whole, which is shorter than its diff:
```python
import math

import jax
import jax.numpy as jnp
from jax import lax
from jax.experimental import pallas as pl
from jax.experimental.pallas import tpu as pltpu
from jax.sharding import PartitionSpec as P

D = 8192
TOKENS = 3584
PANEL = 128
DAMPING = 0.01
MESH = pl.DeviceIdType.MESH
F32, BF16 = jnp.float32, jnp.bfloat16
HIGHEST = lax.Precision.HIGHEST

N_SENT = 32
N_RECEIVED = 92


def dot(a, b, dims, precision=None):
    return lax.dot_general(a, b, (dims, ((), ())), precision=precision, preferred_element_type=F32)


def rel(i, o):
    return lax.rem(i + o, 4)


def kernel(
    a_hbm, c_hbm, q_hbm, v_hbm, f_hbm, p_hbm, upd_ref, new_ref,
    q, f, v, act, rot, cot, pan, scale, moment,
    send_c, recv_c, out2, recv2, out1p, out1m, recv1m, recv1p, out_z, recv_z, total, s, acc,
    im_part, im_c, im_s, im_x, im_xs, im_z,
    gr, gr_c, gr_h, gr_x, gr_q, gr_l, gr_l2, gr_y, gr_y2, gr_z, gr_full, chol,
    send_sem, recv_sem, local_sem,
):
    grp, dev = lax.axis_index("grp"), lax.axis_index("dev")
    y, h = grp // 4, lax.rem(grp, 4)
    c = lax.rem(dev, 2)
    x = lax.rem(dev // 2, 4)
    z = dev // 8
    other = 1 - c

    def at(yy=y, hh=h, zz=z, xx=x, cc=c):
        return (yy * 4 + hh, (zz * 4 + xx) * 2 + cc)

    core_peer = at(cc=other)
    x_peer = {o: at(xx=rel(x, o)) for o in (1, 2, 3)}
    z_peer = {o: at(zz=rel(z, o)) for o in (1, 2, 3)}
    y_peer = {o: at(yy=rel(y, o)) for o in (1, 2, 3)}
    h_peer = {o: at(hh=rel(h, o)) for o in (1, 2, 3)}
    peers = [core_peer]
    for table in (x_peer, z_peer, y_peer, h_peer):
        peers += [table[o] for o in (1, 2, 3)]

    barrier = pltpu.get_barrier_semaphore()
    for peer in peers:
        pl.semaphore_signal(barrier, inc=1, device_id=peer, device_id_type=MESH)

    pairs = (
        (p_hbm, pan.at[h, y]), (c_hbm, cot.at[x, z, c]), (a_hbm, act), (q_hbm, q),
        (f_hbm, f), (v_hbm, v),
    )
    loads = [pltpu.make_async_copy(src, dst, local_sem.at[n]) for n, (src, dst) in enumerate(pairs)]
    for load in loads:
        load.start()
    for load in loads[:2]:
        load.wait()
    pl.semaphore_wait(barrier, len(peers))

    sent, received = {}, {}

    def push(group, key, src, dst, peer):
        copy = pltpu.make_async_remote_copy(
            src_ref=src, dst_ref=dst,
            send_sem=send_sem.at[sent.setdefault(group, [len(sent), 0])[0]],
            recv_sem=recv_sem.at[received.setdefault((group, key), [len(received), 0])[0]],
            device_id=peer, device_id_type=MESH,
        )
        copy.start()
        size = math.prod(src.shape) * src.dtype.itemsize
        sent[group][1] += size
        received[group, key][1] += size

    def wait_bytes(semaphore, entry, like):
        assert entry[1] == math.prod(like.shape) * like.dtype.itemsize
        entry[1] = 0
        pltpu.make_async_copy(like, like, semaphore.at[entry[0]]).wait()

    def need(group, key, like):
        wait_bytes(recv_sem, received[group, key], like)

    def cot_push(group, key, xx, zz, peer):
        push(group, key, cot.at[xx, zz, c], cot.at[xx, zz, c], peer)

    def cot_forward(j):
        need("cot_x", j, cot.at[0, 0:2, 0])
        o = 1 if j < 2 else 3
        cot_push("cot_f", 0, rel(x, 4 - o), rel(z, j), x_peer[o])

    def cot_pair(o):
        part = cot.at[rel(x, o), :, c]
        push("cot_c", 0, part, part, core_peer)

    order = (2, 1, 3, 0)

    def columns(k, oz, ox, cc):
        start = ((rel(z, oz) * 4 + rel(x, ox)) * 2 + cc) * 256 + k * 128
        return q[:, pl.ds(pl.multiple_of(start, 128), 128)]

    def block(k, ox, j, cc):
        return dot(act[...], columns(k, order[j], ox, cc), ((1,), (0,)))

    def send_core(k):
        for ox in (2, 3, 1, 0):
            for j in range(4):
                send_c[k, ox, j] = block(k, ox, j, other).astype(BF16)
            push("core", (k, ox), send_c.at[k, ox], recv_c.at[k, ox], core_peer)

    def pair_sum(k, ox, j):
        return block(k, ox, j, c) + recv_c[k, ox, j].astype(F32)

    def send_far(k, j):
        out2[k, j] = pair_sum(k, 2, j).astype(BF16)
        push("far", (k, j), out2.at[k, j], recv2.at[k, j], x_peer[1 if j < 2 else 3])

    def send_plus(k, j):
        total_j = pair_sum(k, 1, j)
        if j < 2:
            need("far", (k, j), recv2.at[k, j])
            total_j = total_j + recv2[k, j].astype(F32)
        out1p[k, j] = total_j.astype(BF16)
        push("near_x", (k, j), out1p.at[k, j], recv1m.at[k, j], x_peer[1])

    def send_minus(k, j):
        total_j = pair_sum(k, 3, j)
        if j >= 2:
            need("far", (k, j), recv2.at[k, j])
            total_j = total_j + recv2[k, j].astype(F32)
        out1m[k, j] = total_j.astype(BF16)
        push("near_x", (k, j), out1m.at[k, j], recv1p.at[k, j], x_peer[3])

    def send_first(k):
        need("core", (k, 2), recv_c.at[k, 2])
        for j in (0, 2, 1, 3):
            send_far(k, j)
        need("core", (k, 3), recv_c.at[k, 3])
        send_minus(k, 0)
        send_minus(k, 1)
        need("core", (k, 1), recv_c.at[k, 1])
        send_plus(k, 2)
        send_plus(k, 3)

    def send_second(k):
        send_plus(k, 0)
        send_minus(k, 2)
        send_plus(k, 1)
        send_minus(k, 3)

    def send_z(k):
        need("core", (k, 0), recv_c.at[k, 0])
        for j in range(4):
            total_j = pair_sum(k, 0, j)
            need("near_x", (k, j), recv1m.at[k, 0:2])
            total_j = total_j + recv1m[k, j].astype(F32) + recv1p[k, j].astype(F32)
            if order[j]:
                out_z[k, j] = total_j.astype(BF16)
                push("near_z", k, out_z.at[k, j], recv_z.at[k, j], z_peer[order[j]])
            else:
                total[k] = total_j

    def rot_to_y(k, j):
        block_j = rot.at[k, rel(h, j), y]
        for o in (2, 1, 3):
            push("rot_y", (k, j), block_j, block_j, y_peer[o])

    def rot_own(k):
        need("near_z", k, recv_z.at[k])
        sum_k = total[k]
        for j in range(3):
            sum_k = sum_k + recv_z[k, j].astype(F32)
        rot[k, h, y] = sum_k.astype(BF16)
        for o in (1, 3):
            push("rot_h", (k, o), rot.at[k, h, y], rot.at[k, h, y], h_peer[o])
        rot_to_y(k, 0)

    def rot_next(k):
        for o in (1, 3):
            need("rot_h", (k, o), rot.at[k, 0, 0])
            lo = 0 if o == 1 else 112
            part = rot.at[k, rel(h, 4 - o), y, lo : lo + 112]
            push("rot_h", (k, 2), part, part, h_peer[o])
            rot_to_y(k, 4 - o)

    def rot_last(k):
        need("rot_h", (k, 2), rot.at[k, 0, 0])
        rot_to_y(k, 2)

    def add_tokens(k, j):
        need("rot_y", (k, j), rot.at[k, 0, 0:3])
        hh = rel(h, j)
        part = dot(rot[k, hh].reshape(896, 128), cot[hh].reshape(896, 256), ((0,), (0,)))
        if j == 0:
            moment[k] = part
        else:
            moment[k] += part

    def gather_own(k):
        s[k, 0, 0, c] = (moment[k] * scale[k * 128 : (k + 1) * 128, :]).astype(BF16)
        mine = s.at[k, 0, 0, c]
        for o in (2, 1, 3):
            push("s_z", (k, o), mine, s.at[k, 0, 4 - o, c], z_peer[o])
        for o in (1, 3):
            push("s_x", (k, 0), mine, s.at[k, 4 - o, 0, c], x_peer[o])

    def gather_z(k, o):
        need("s_z", (k, o), s.at[k, 0, 0, 0])
        j = 4 - o
        for ox in (1, 3):
            push("s_x", (k, j), s.at[k, 0, j, c], s.at[k, 4 - ox, j, c], x_peer[ox])

    def gather_pair(k, ox, lo, hi):
        part = s.at[k, ox, lo:hi, c]
        push("s_c", (k, ox, lo), part, part, core_peer)

    def gather_forward(k, j):
        need("s_x", (k, j), s.at[k, 0, 0:2, 0])
        o = 1 if j < 2 else 3
        push("s_f", (k, j // 2), s.at[k, 4 - o, j, c], s.at[k, 2, j, c], x_peer[o])

    def add_blocks(k, ox, lo, hi):
        need("s_c", (k, ox, lo), s.at[k, 0, 0 : hi - lo, 0])
        sum_j = jnp.zeros((256, 256), F32)
        for j in range(lo, hi):
            for cc in (0, 1):
                sum_j = sum_j + dot(columns(k, j, ox, cc), s[k, ox, j, cc], ((1,), (0,)))
        if k == 0 and ox == 0:
            acc[...] = sum_j
        else:
            acc[...] += sum_j

    lane = lax.broadcasted_iota(jnp.int32, (16, 2 * PANEL), 1)
    row = lax.broadcasted_iota(jnp.int32, (16, 2 * PANEL), 0)

    def eliminate(b):
        k0 = 16 * b
        r = chol[k0 : k0 + 16, :]
        for i in range(16):
            column = r[:, k0 + i : k0 + i + 1]
            pivot = column[i : i + 1, :]
            inv = lax.rsqrt(pivot)
            inv = inv * (1.5 - 0.5 * pivot * inv * inv)
            below = column * inv
            r_row = r[i : i + 1, :] * inv
            r = jnp.where(row == i, r_row, jnp.where(row > i, r - below * r_row, r))
        chol[k0 : k0 + 16, :] = r
        if b < 7:
            r = jnp.where(lane >= k0 + 16, r, 0.0)
            hi = r.astype(BF16)
            rest = r - hi.astype(F32)
            mid = rest.astype(BF16)
            low = (rest - mid.astype(F32)).astype(BF16)
            left = jnp.concatenate([hi, hi, hi, mid, mid, low], axis=0)[:, :PANEL]
            right = jnp.concatenate([hi, mid, low, hi, mid, hi], axis=0)
            chol[k0 + 16 :, :] -= dot(left, right, ((0,), (0,)))[k0 + 16 :, :]

    def panel_y():
        need("pan_h", 0, pan.at[0, 0:3])
        for o in (1, 2, 3):
            push("pan_y", 0, pan.at[:, y], pan.at[:, y], y_peer[o])

    def image_core():
        need("pan_y", 0, pan.at[0:3])
        loads[4].wait()
        pan_t = pan[...].transpose(1, 0, 2, 3).reshape(PANEL, 256)
        im_part[...] = dot(f[...], pan_t, ((1,), (1,)), HIGHEST).reshape(4, 4, 2, 16, PANEL)
        push("im_core", 0, im_part.at[:, :, other], im_c, core_peer)

    def image_x():
        need("im_core", 0, im_c)
        im_s[...] = im_part[:, :, c] + im_c[...]
        for o in (1, 2, 3):
            push("im_xc", 0, im_s.at[:, rel(x, o)], im_x.at[o], x_peer[o])

    def image_z():
        need("im_xc", 0, im_x.at[1:4])
        im_xs[...] = im_s[:, x] + im_x[1] + im_x[2] + im_x[3]
        for o in (1, 2, 3):
            push("im_zc", 0, im_xs.at[rel(z, o)], im_z.at[o], z_peer[o])

    def gram_core():
        need("im_zc", 0, im_z.at[1:4])
        image = im_xs[z] + im_z[1] + im_z[2] + im_z[3]
        gr[...] = dot(image, image, ((0,), (0,)), HIGHEST) * (1.0 / D)
        chol[:, PANEL:] = jnp.concatenate([image, jnp.zeros((PANEL - 16, PANEL), F32)], axis=0).T
        push("gr_core", 0, gr.at[pl.ds(pl.multiple_of(other * 64, 64), 64)], gr_c, core_peer)

    def gram_x():
        need("gr_core", 0, gr_c)
        gr_h[...] = gr[pl.ds(pl.multiple_of(c * 64, 64), 64), :] + gr_c[...]
        for o in (1, 2, 3):
            share = pl.ds(pl.multiple_of(rel(x, o) * 16, 16), 16)
            push("gr_xc", 0, gr_h.at[share], gr_x.at[o], x_peer[o])

    def gram_z():
        need("gr_xc", 0, gr_x.at[1:4])
        mine = gr_h[pl.ds(pl.multiple_of(x * 16, 16), 16), :]
        gr_q[...] = mine + gr_x[1] + gr_x[2] + gr_x[3]
        for o in (1, 2, 3):
            push("gr_zc", 0, gr_q, gr_l.at[o], z_peer[o])

    def gram_y():
        need("gr_zc", 0, gr_l.at[1:4])
        gr_l2[...] = gr_q[...] + gr_l[1] + gr_l[2] + gr_l[3]
        for o in (1, 2, 3):
            push("gr_yc", 0, gr_l2, gr_y.at[o], y_peer[o])

    def gram_h():
        need("gr_yc", 0, gr_y.at[1:4])
        gr_y2[...] = gr_l2[...] + gr_y[1] + gr_y[2] + gr_y[3]
        for o in (1, 2, 3):
            push("gr_hc", 0, gr_y2, gr_z.at[o], h_peer[o])

    def gram_x_back():
        need("gr_hc", 0, gr_z.at[1:4])
        lo = pl.ds(pl.multiple_of(c * 64 + x * 16, 16), 16)
        gr_full[lo, :] = gr_y2[...] + gr_z[1] + gr_z[2] + gr_z[3]
        for o in (1, 2, 3):
            push("gr_xg", 0, gr_full.at[lo], gr_full.at[lo], x_peer[o])

    def gram_core_back():
        need("gr_xg", 0, gr_full.at[0:48])
        half = pl.ds(pl.multiple_of(c * 64, 64), 64)
        push("gr_cg", 0, gr_full.at[half], gr_full.at[half], core_peer)

    for o in (2, 1, 3):
        push("pan_h", 0, pan.at[h, y], pan.at[h, y], h_peer[o])
    for o in (2, 1, 3):
        cot_push("cot_z", o, x, z, z_peer[o])
    loads[2].wait()
    loads[3].wait()
    send_core(0)
    send_first(0)
    send_core(1)
    loads[5].wait()
    scale[...] = (1.0 / TOKENS) / (v[...].astype(F32) + DAMPING)
    panel_y()
    send_second(0)
    send_first(1)
    image_core()
    send_z(0)
    image_x()
    send_second(1)
    for o in (1, 3):
        cot_push("cot_x", 0, x, z, x_peer[o])
    for o in (1, 3, 2):
        need("cot_z", o, cot.at[0, 0, 0])
        for ox in (1, 3):
            cot_push("cot_x", 4 - o, x, rel(z, 4 - o), x_peer[ox])
    cot_pair(0)
    image_z()
    rot_own(0)
    gram_core()
    send_z(1)
    gram_x()
    for j in (0, 3, 1, 2):
        cot_forward(j)
    cot_pair(1)
    cot_pair(3)
    gram_z()
    rot_next(0)
    gram_y()
    rot_own(1)
    need("cot_f", 0, cot.at[:, 0, 0])
    cot_pair(2)
    gram_h()
    rot_last(0)
    need("cot_c", 0, cot.at[:, :, 0])
    rot_next(1)
    for j in (0, 3, 1, 2):
        add_tokens(0, j)
    gather_own(0)
    gram_x_back()
    rot_last(1)
    gather_z(0, 1)
    gather_z(0, 3)
    gram_core_back()
    gather_z(0, 2)
    gather_pair(0, 0, 0, 4)
    need("gr_cg", 0, gr_full.at[0:64])
    chol[:, :PANEL] = gr_full[...]
    eliminate(0)
    for j in (0, 3, 1, 2):
        add_tokens(1, j)
    gather_own(1)
    gather_forward(0, 0)
    gather_forward(0, 3)
    eliminate(1)
    gather_forward(0, 1)
    gather_forward(0, 2)
    gather_pair(0, 1, 0, 4)
    gather_pair(0, 3, 0, 4)
    eliminate(2)
    gather_z(1, 1)
    gather_z(1, 3)
    eliminate(3)
    gather_z(1, 2)
    gather_pair(1, 0, 0, 4)
    need("s_f", (0, 0), s.at[0, 0, 0:2, 0])
    gather_pair(0, 2, 0, 2)
    need("s_f", (0, 1), s.at[0, 0, 0:2, 0])
    gather_pair(0, 2, 2, 4)
    eliminate(4)
    gather_forward(1, 0)
    gather_forward(1, 3)
    add_blocks(0, 0, 0, 4)
    eliminate(5)
    gather_forward(1, 1)
    gather_forward(1, 2)
    gather_pair(1, 1, 0, 4)
    gather_pair(1, 3, 0, 4)
    add_blocks(0, 1, 0, 4)
    add_blocks(0, 3, 0, 4)
    add_blocks(0, 2, 0, 2)
    add_blocks(0, 2, 2, 4)
    add_blocks(1, 0, 0, 4)
    eliminate(6)
    need("s_f", (1, 0), s.at[1, 0, 0:2, 0])
    gather_pair(1, 2, 0, 2)
    need("s_f", (1, 1), s.at[1, 0, 0:2, 0])
    gather_pair(1, 2, 2, 4)
    eliminate(7)
    new_ref[...] = chol[:, PANEL:].T[:16, :]
    add_blocks(1, 1, 0, 4)
    add_blocks(1, 3, 0, 4)
    add_blocks(1, 2, 0, 2)
    add_blocks(1, 2, 2, 4)
    upd_ref[...] = acc[...].astype(BF16)
    bytes_like = {
        "pan_h": pan.at[0, 0:3], "pan_y": pan.at[0:3], "im_core": im_c, "im_xc": im_x.at[1:4],
        "im_zc": im_z.at[1:4], "gr_core": gr_c, "gr_xc": gr_x.at[1:4], "gr_zc": gr_l.at[1:4],
        "gr_yc": gr_y.at[1:4], "gr_hc": gr_z.at[1:4], "gr_xg": gr_full.at[0:48],
        "gr_cg": gr_full.at[0:64], "cot_z": cot.at[0, 0:3, 0], "cot_x": cot.at[:, 0:2, 0],
        "cot_f": cot.at[:, 0, 0], "cot_c": cot.at[:, :, 0], "core": send_c, "far": out2,
        "near_x": send_c.at[:, 0:2], "near_z": out_z, "rot_h": rot.at[:, 0, 0:3],
        "rot_y": rot.at[:, 0:3], "s_z": s.at[:, 0, 0:3, 0], "s_x": s.at[:, 0:2, :, 0],
        "s_f": s.at[:, 0, :, 0], "s_c": s.at[:, :, :, 0],
    }
    for group, entry in sent.items():
        wait_bytes(send_sem, entry, bytes_like[group])
    assert len(sent) <= N_SENT and len(received) <= N_RECEIVED
    assert not any(size for _, size in received.values())


def body(activations, cotangent, eigenbasis, second_moment, factor, old_panel):
    vmem = pl.BlockSpec(memory_space=pltpu.VMEM)
    hbm = pl.BlockSpec(memory_space=pl.ANY)
    tile = (224, 128)
    half = (128, 256)
    part = (16, PANEL)
    scratch = [
        pltpu.VMEM((256, D), BF16),
        pltpu.VMEM((512, 256), F32),
        pltpu.VMEM((256, 256), BF16),
        pltpu.VMEM((224, 256), BF16),
        pltpu.VMEM((2, 4, 4) + tile, BF16),
        pltpu.VMEM((4, 4, 2, 112, 256), BF16),
        pltpu.VMEM((4, 4, 8, 256), F32),
        pltpu.VMEM((256, 256), F32),
        pltpu.VMEM((2,) + half, F32),
        pltpu.VMEM((2, 4, 4) + tile, BF16),
        pltpu.VMEM((2, 4, 4) + tile, BF16),
        pltpu.VMEM((2, 4) + tile, BF16),
        pltpu.VMEM((2, 4) + tile, BF16),
        pltpu.VMEM((2, 4) + tile, BF16),
        pltpu.VMEM((2, 4) + tile, BF16),
        pltpu.VMEM((2, 4) + tile, BF16),
        pltpu.VMEM((2, 4) + tile, BF16),
        pltpu.VMEM((2, 3) + tile, BF16),
        pltpu.VMEM((2, 3) + tile, BF16),
        pltpu.VMEM((2,) + tile, F32),
        pltpu.VMEM((2, 4, 4, 2) + half, BF16),
        pltpu.VMEM((256, 256), F32),
        pltpu.VMEM((4, 4, 2) + part, F32),
        pltpu.VMEM((4, 4) + part, F32),
        pltpu.VMEM((4, 4) + part, F32),
        pltpu.VMEM((4, 4) + part, F32),
        pltpu.VMEM((4,) + part, F32),
        pltpu.VMEM((4,) + part, F32),
        pltpu.VMEM((PANEL, PANEL), F32),
        pltpu.VMEM((64, PANEL), F32),
        pltpu.VMEM((64, PANEL), F32),
        pltpu.VMEM((4,) + part, F32),
        pltpu.VMEM(part, F32),
        pltpu.VMEM((4,) + part, F32),
        pltpu.VMEM(part, F32),
        pltpu.VMEM((4,) + part, F32),
        pltpu.VMEM(part, F32),
        pltpu.VMEM((4,) + part, F32),
        pltpu.VMEM((PANEL, PANEL), F32),
        pltpu.VMEM((PANEL, 2 * PANEL), F32),
        pltpu.SemaphoreType.DMA((N_SENT,)),
        pltpu.SemaphoreType.DMA((N_RECEIVED,)),
        pltpu.SemaphoreType.DMA((6,)),
    ]
    return pl.pallas_call(
        kernel,
        out_shape=(
            jax.ShapeDtypeStruct((256, 256), BF16),
            jax.ShapeDtypeStruct(part, F32),
        ),
        in_specs=[hbm] * 6,
        out_specs=(vmem, vmem),
        scratch_shapes=scratch,
        compiler_params=pltpu.CompilerParams(
            collective_id=0, has_side_effects=True, vmem_limit_bytes=60 * 1024 * 1024
        ),
    )(
        activations, cotangent, eigenbasis, second_moment, factor, old_panel.T
    )


def solution(mesh):
    return jax.shard_map(
        body,
        mesh=mesh,
        in_specs=(
            P("grp", "dev"),
            P("dev", "grp"),
            P("dev", None),
            P("dev", "grp"),
            P("grp", "dev"),
            P("dev", "grp"),
        ),
        out_specs=(P("dev", "grp"), P(("grp", "dev"), None)),
        check_vma=False,
    )
```

time: 105 us -> 97.5 us (0.929)
  the two profiles are of different devices: /device:TPU:93 before, /device:TPU:1 now
where the time goes in v4:
time: 97.5 us; the launch traced here: 97.3 us
  Pallas kernels  93.8 us (96%)
  local copies, waits for them, and re-layouts  2.86 us (3%)
    pallas_call x1, Pallas kernels, body(): pl.pallas_call(kernel, out_shape=(jax.ShapeDtypeStruct((256, 256), BF16),...  93.8 us
    unnamed x2, local copies, waits for them, and re-layouts  2.86 us

profile of v4, /device:TPU:1, one launch (start us, length us, event | category | flops | bytes accessed | tf_op | source)
XLA Modules:
  0.0 97.3 jit_solution(2542284081393266818)
XLA Ops:
  0.6 93.8 %shard_map.77 = (bf16[256,256]{1,0:T(8,128)(2,1)}, f32[16,128]{1,0:T(8,128)}) custom-call(bf16[224,256]{1,0:T(8,128)(2,1)} %a_hbm.1, bf16[112,256]{1,0:T(8,128)(2,1)} %c_hbm.1, bf16[256,8192]{1,0:T(8,128)(2,1)} %q_hbm.1, bf16[256,256]{1,0:T(8,128)(2,1)} %v_hbm.1, f32[512,256]{1,0:T(8,128)} %f_hbm.1, f32[8,256]{1,0:T(8,128)} %bitcast.1), custom_call_target="tpu_custom_call" | custom-call | tf_op jit(solution)/shard_map/pallas_call | solution.py:507
  94.4 1.6 %copy.10 = bf16[256,256]{1,0:T(8,128)(2,1)} copy(bf16[256,256]{1,0:T(8,128)(2,1)} %get-tuple-element.4) | data formatting | bytes 262144
  96.0 1.3 %copy.11 = f32[16,128]{1,0:T(8,128)} copy(f32[16,128]{1,0:T(8,128)} %get-tuple-element.5) | data formatting | bytes 16384

commit v5 on v4

--- a/solution.py
+++ b/solution.py
@@ -241,19 +241,25 @@
             acc[...] += sum_j
 
     lane = lax.broadcasted_iota(jnp.int32, (16, 2 * PANEL), 1)
-    row = lax.broadcasted_iota(jnp.int32, (16, 2 * PANEL), 0)
+    row = lax.broadcasted_iota(jnp.int32, (16, PANEL), 0)
 
     def eliminate(b):
         k0 = 16 * b
-        r = chol[k0 : k0 + 16, :]
+        left = chol[k0 : k0 + 16, :PANEL]
+        right = chol[k0 : k0 + 16, PANEL:]
+        wide = [jnp.broadcast_to(left[:, k0 + j : k0 + j + 1], (16, PANEL)) for j in range(16)]
         for i in range(16):
-            column = r[:, k0 + i : k0 + i + 1]
-            pivot = column[i : i + 1, :]
+            pivot = wide[i][i : i + 1, :]
             inv = lax.rsqrt(pivot)
             inv = inv * (1.5 - 0.5 * pivot * inv * inv)
-            below = column * inv
-            r_row = r[i : i + 1, :] * inv
-            r = jnp.where(row == i, r_row, jnp.where(row > i, r - below * r_row, r))
+            below = jnp.where(row > i, wide[i] * inv, 0.0)
+            for j in range(i + 1, 16):
+                wide[j] = wide[j] - below * (wide[j][i : i + 1, :] * inv)
+            left_row = left[i : i + 1, :] * inv
+            right_row = right[i : i + 1, :] * inv
+            left = jnp.where(row == i, left_row, left - below * left_row)
+            right = jnp.where(row == i, right_row, right - below * right_row)
+        r = jnp.concatenate([left, right], axis=1)
         chol[k0 : k0 + 16, :] = r
         if b < 7:
             r = jnp.where(lane >= k0 + 16, r, 0.0)
@@ -261,9 +267,9 @@
             rest = r - hi.astype(F32)
             mid = rest.astype(BF16)
             low = (rest - mid.astype(F32)).astype(BF16)
-            left = jnp.concatenate([hi, hi, hi, mid, mid, low], axis=0)[:, :PANEL]
-            right = jnp.concatenate([hi, mid, low, hi, mid, hi], axis=0)
-            chol[k0 + 16 :, :] -= dot(left, right, ((0,), (0,)))[k0 + 16 :, :]
+            first = jnp.concatenate([hi, hi, hi, mid, mid, low], axis=0)[:, :PANEL]
+            second = jnp.concatenate([hi, mid, low, hi, mid, hi], axis=0)
+            chol[k0 + 16 :, :] -= dot(first, second, ((0,), (0,)))[k0 + 16 :, :]
 
     def panel_y():
         need("pan_h", 0, pan.at[0, 0:3])
@@ -348,10 +354,10 @@
     panel_y()
     send_second(0)
     send_first(1)
+    send_z(0)
     image_core()
-    send_z(0)
+    send_second(1)
     image_x()
-    send_second(1)
     for o in (1, 3):
         cot_push("cot_x", 0, x, z, x_peer[o])
     for o in (1, 3, 2):
@@ -359,63 +365,63 @@
         for ox in (1, 3):
             cot_push("cot_x", 4 - o, x, rel(z, 4 - o), x_peer[ox])
     cot_pair(0)
+    rot_own(0)
     image_z()
-    rot_own(0)
-    gram_core()
     send_z(1)
-    gram_x()
     for j in (0, 3, 1, 2):
         cot_forward(j)
     cot_pair(1)
     cot_pair(3)
-    gram_z()
+    gram_core()
     rot_next(0)
-    gram_y()
+    gram_x()
     rot_own(1)
     need("cot_f", 0, cot.at[:, 0, 0])
     cot_pair(2)
-    gram_h()
+    gram_z()
     rot_last(0)
+    gram_y()
     need("cot_c", 0, cot.at[:, :, 0])
     rot_next(1)
     for j in (0, 3, 1, 2):
         add_tokens(0, j)
     gather_own(0)
-    gram_x_back()
+    gram_h()
     rot_last(1)
     gather_z(0, 1)
     gather_z(0, 3)
-    gram_core_back()
     gather_z(0, 2)
     gather_pair(0, 0, 0, 4)
-    need("gr_cg", 0, gr_full.at[0:64])
-    chol[:, :PANEL] = gr_full[...]
-    eliminate(0)
     for j in (0, 3, 1, 2):
         add_tokens(1, j)
     gather_own(1)
+    gram_x_back()
     gather_forward(0, 0)
     gather_forward(0, 3)
-    eliminate(1)
     gather_forward(0, 1)
     gather_forward(0, 2)
     gather_pair(0, 1, 0, 4)
     gather_pair(0, 3, 0, 4)
-    eliminate(2)
+    gram_core_back()
     gather_z(1, 1)
     gather_z(1, 3)
-    eliminate(3)
+    need("gr_cg", 0, gr_full.at[0:64])
+    chol[:, :PANEL] = gr_full[...]
     gather_z(1, 2)
     gather_pair(1, 0, 0, 4)
+    eliminate(0)
+    eliminate(1)
     need("s_f", (0, 0), s.at[0, 0, 0:2, 0])
     gather_pair(0, 2, 0, 2)
     need("s_f", (0, 1), s.at[0, 0, 0:2, 0])
     gather_pair(0, 2, 2, 4)
-    eliminate(4)
+    eliminate(2)
+    eliminate(3)
     gather_forward(1, 0)
     gather_forward(1, 3)
+    eliminate(4)
+    eliminate(5)
     add_blocks(0, 0, 0, 4)
-    eliminate(5)
     gather_forward(1, 1)
     gather_forward(1, 2)
     gather_pair(1, 1, 0, 4)

time: 97.5 us -> 89.2 us (0.915)
  Pallas kernels: 93.8 us -> 85.5 us
    pallas_call x1, Pallas kernels: 93.8 us -> 85.5 us  [body(): pl.pallas_call(kernel, out_shape=(jax.ShapeDtypeStruct((256, 256), BF16),...]
where the time goes in v5:
time: 89.2 us; the launch traced here: 89 us
  Pallas kernels  85.5 us (96%)
  local copies, waits for them, and re-layouts  2.86 us (3%)
    pallas_call x1, Pallas kernels, body(): pl.pallas_call(kernel, out_shape=(jax.ShapeDtypeStruct((256, 256), BF16),...  85.5 us
    unnamed x2, local copies, waits for them, and re-layouts  2.86 us

profile of v5, /device:TPU:1, one launch (start us, length us, event | category | flops | bytes accessed | tf_op | source)
XLA Modules:
  0.0 89.0 jit_solution(5215643564680749938)
XLA Ops:
  0.6 85.5 %shard_map.77 = (bf16[256,256]{1,0:T(8,128)(2,1)}, f32[16,128]{1,0:T(8,128)}) custom-call(bf16[224,256]{1,0:T(8,128)(2,1)} %a_hbm.1, bf16[112,256]{1,0:T(8,128)(2,1)} %c_hbm.1, bf16[256,8192]{1,0:T(8,128)(2,1)} %q_hbm.1, bf16[256,256]{1,0:T(8,128)(2,1)} %v_hbm.1, f32[512,256]{1,0:T(8,128)} %f_hbm.1, f32[8,256]{1,0:T(8,128)} %bitcast.1), custom_call_target="tpu_custom_call" | custom-call | tf_op jit(solution)/shard_map/pallas_call | solution.py:513
  86.1 1.6 %copy.10 = bf16[256,256]{1,0:T(8,128)(2,1)} copy(bf16[256,256]{1,0:T(8,128)(2,1)} %get-tuple-element.4) | data formatting | bytes 262144
  87.7 1.3 %copy.11 = f32[16,128]{1,0:T(8,128)} copy(f32[16,128]{1,0:T(8,128)} %get-tuple-element.5) | data formatting | bytes 16384

commit v6 on v5

--- a/solution.py
+++ b/solution.py
@@ -15,8 +15,8 @@
 F32, BF16 = jnp.float32, jnp.bfloat16
 HIGHEST = lax.Precision.HIGHEST
 
-N_SENT = 32
-N_RECEIVED = 92
+N_SENT = 26
+N_RECEIVED = 89
 
 
 def dot(a, b, dims, precision=None):
@@ -59,7 +59,8 @@
         pl.semaphore_signal(barrier, inc=1, device_id=peer, device_id_type=MESH)
 
     pairs = (
-        (p_hbm, pan.at[h, y]), (c_hbm, cot.at[x, z, c]), (a_hbm, act), (q_hbm, q),
+        (p_hbm, pan.at[h, y]), (c_hbm, cot.at[x, z, c]), (a_hbm, act),
+        *((q_hbm.at[n : n + 64], q.at[n : n + 64]) for n in range(0, 256, 64)),
         (f_hbm, f), (v_hbm, v),
     )
     loads = [pltpu.make_async_copy(src, dst, local_sem.at[n]) for n, (src, dst) in enumerate(pairs)]
@@ -278,7 +279,7 @@
 
     def image_core():
         need("pan_y", 0, pan.at[0:3])
-        loads[4].wait()
+        loads[7].wait()
         pan_t = pan[...].transpose(1, 0, 2, 3).reshape(PANEL, 256)
         im_part[...] = dot(f[...], pan_t, ((1,), (1,)), HIGHEST).reshape(4, 4, 2, 16, PANEL)
         push("im_core", 0, im_part.at[:, :, other], im_c, core_peer)
@@ -344,12 +345,12 @@
         push("pan_h", 0, pan.at[h, y], pan.at[h, y], h_peer[o])
     for o in (2, 1, 3):
         cot_push("cot_z", o, x, z, z_peer[o])
-    loads[2].wait()
-    loads[3].wait()
+    for load in loads[2:7]:
+        load.wait()
     send_core(0)
     send_first(0)
     send_core(1)
-    loads[5].wait()
+    loads[8].wait()
     scale[...] = (1.0 / TOKENS) / (v[...].astype(F32) + DAMPING)
     panel_y()
     send_second(0)
@@ -508,7 +509,7 @@
         pltpu.VMEM((PANEL, 2 * PANEL), F32),
         pltpu.SemaphoreType.DMA((N_SENT,)),
         pltpu.SemaphoreType.DMA((N_RECEIVED,)),
-        pltpu.SemaphoreType.DMA((6,)),
+        pltpu.SemaphoreType.DMA((9,)),
     ]
     return pl.pallas_call(
         kernel,

time: 89.2 us -> 89.6 us (level)
  no operation moved by 1% of the time
where the time goes in v6:
time: 89.6 us; the launch traced here: 89.4 us
  Pallas kernels  85.9 us (96%)
  local copies, waits for them, and re-layouts  2.86 us (3%)
    pallas_call x1, Pallas kernels, body(): pl.pallas_call(kernel, out_shape=(jax.ShapeDtypeStruct((256, 256), BF16),...  85.9 us
    unnamed x2, local copies, waits for them, and re-layouts  2.86 us

profile of v6, /device:TPU:1, one launch (start us, length us, event | category | flops | bytes accessed | tf_op | source)
XLA Modules:
  0.0 89.4 jit_solution(11462070222547177564)
XLA Ops:
  0.6 85.9 %shard_map.77 = (bf16[256,256]{1,0:T(8,128)(2,1)}, f32[16,128]{1,0:T(8,128)}) custom-call(bf16[224,256]{1,0:T(8,128)(2,1)} %a_hbm.1, bf16[112,256]{1,0:T(8,128)(2,1)} %c_hbm.1, bf16[256,8192]{1,0:T(8,128)(2,1)} %q_hbm.1, bf16[256,256]{1,0:T(8,128)(2,1)} %v_hbm.1, f32[512,256]{1,0:T(8,128)} %f_hbm.1, f32[8,256]{1,0:T(8,128)} %bitcast.1), custom_call_target="tpu_custom_call" | custom-call | tf_op jit(solution)/shard_map/pallas_call | solution.py:514
  86.5 1.6 %copy.10 = bf16[256,256]{1,0:T(8,128)(2,1)} copy(bf16[256,256]{1,0:T(8,128)(2,1)} %get-tuple-element.4) | data formatting | bytes 262144
  88.1 1.3 %copy.11 = f32[16,128]{1,0:T(8,128)} copy(f32[16,128]{1,0:T(8,128)} %get-tuple-element.5) | data formatting | bytes 16384
